TPU v7x, 512 devices: a whole 4x4x16 slice. The times are simulated.
512 devices in a mesh: gen: 16 (over z), train: 32 (over x, y, core).
Axes of the slice: x: 4, y: 4, z: 16, core: 2. Of those that a mesh axis runs over, the one named last changes fastest.
Arguments:
- gen_embed: float32 [16384, 256], P(('gen', 'train')), may hold values from -20 to 20, as said below
- train_embed: float32 [16384, 256], P(('train', 'gen')), may hold values from -20 to 20, as said below
- row_mass: float32 [16384], P('gen'), may hold values from 1 to 100, as said below
- col_mass: float32 [16384], P('train'), may hold values from 1 to 100, as said below
Outputs:
- row_potential: float32 [16384], P('gen')
- col_potential: float32 [16384], P('train')
- transport_cost: float32 [], replicated
Inputs may be any that keep to these rules, and one draw needn't show every extreme that they name: `gen_embed`: finite embeddings. `train_embed`: finite embeddings. `row_mass`: positive masses. `col_mass`: positive masses.
All inputs are finite; a program needn't handle non-finite values.
Results may differ from a plain program's by a relative error of at most 0.0003.
Values sent between devices are 32-bit elements; how exact they have to be, the bound alone decides.
No kernel may reach another device: no remote copies, remote signals or barrier semaphores. Data moves between devices by JAX's collectives and lax.ppermute only.
A program may use at most 64 MiB of HBM per device.

v0:
```python
import jax
import jax.numpy as jnp
from jax import lax
from jax.sharding import PartitionSpec as P

ITERS = 3


EPSILON = 0.05


def block_costs(left_rows, right_rows):
    left_sq = jnp.sum(left_rows * left_rows, axis=1)
    right_sq = jnp.sum(right_rows * right_rows, axis=1)
    inner = jnp.dot(
        left_rows, right_rows.T, precision=lax.Precision.HIGHEST, preferred_element_type=jnp.float32
    )
    return (left_sq[:, None] + right_sq[None, :] - 2.0 * inner) / left_rows.shape[1]


def reduce_rows(local_max, local_sum, local_mass):
    highest = lax.pmax(local_max, "train")
    totals, mass_all = lax.psum((local_sum * jnp.exp(local_max - highest), local_mass), "train")
    return (highest, totals, mass_all)


def reduce_cols(local_max, local_sum, local_mass):
    highest = lax.pmax(local_max, "gen")
    totals, mass_all = lax.psum((local_sum * jnp.exp(local_max - highest), local_mass), "gen")
    return (highest, totals, mass_all)


def shards(gen_embed, train_embed, row_mass, col_mass):
    train_block = lax.all_gather(train_embed, "gen", axis=0, tiled=True)
    gen_block = lax.all_gather(gen_embed, "train", axis=0, tiled=True)

    def get_costs():
        return block_costs(gen_block, train_block)

    log_gen_raw = jnp.log(row_mass)
    log_train_raw = jnp.log(col_mass)
    gen_local = jnp.sum(row_mass)
    train_local = jnp.sum(col_mass)
    col_pot = jnp.zeros((col_mass.shape[0],), jnp.float32)
    row_pot = jnp.zeros((row_mass.shape[0],), jnp.float32)
    gen_total = gen_local
    train_total = train_local
    for iteration in range(ITERS):
        costs = get_costs()
        scores = (col_pot[None, :] - costs) / EPSILON + log_train_raw[None, :]
        local_max = jnp.max(scores, axis=1)
        local_sum = jnp.sum(jnp.exp(scores - local_max[:, None]), axis=1)
        highest, totals, train_total = reduce_rows(local_max, local_sum, train_local)
        row_pot = -EPSILON * (highest + jnp.log(totals) - jnp.log(train_total))
        costs = get_costs()
        scores = (row_pot[:, None] - costs) / EPSILON + log_gen_raw[:, None]
        local_max = jnp.max(scores, axis=0)
        local_sum = jnp.sum(jnp.exp(scores - local_max[None, :]), axis=0)
        highest, totals, gen_total = reduce_cols(local_max, local_sum, gen_local)
        col_pot = -EPSILON * (highest + jnp.log(totals) - jnp.log(gen_total))
    costs = get_costs()
    log_gen = log_gen_raw - jnp.log(gen_total)
    log_train = log_train_raw - jnp.log(train_total)
    log_plan = (
        (row_pot[:, None] + col_pot[None, :] - costs) / EPSILON
        + log_gen[:, None]
        + log_train[None, :]
    )
    local_cost = jnp.sum(jnp.exp(log_plan) * costs)
    transport = lax.psum(local_cost, ("gen", "train"))
    return (row_pot, col_pot, transport)


def solution(mesh):
    in_specs = (P(("gen", "train"), None), P(("train", "gen"), None), P("gen"), P("train"))
    out_specs = (P("gen"), P("train"), P())
    return jax.shard_map(shards, mesh=mesh, in_specs=in_specs, out_specs=out_specs, check_vma=False)
```

profile of v0, /device:TPU:1, one launch (start us, length us, event | category | flops | bytes accessed | tf_op | source)
XLA Modules:
  0.0 745.7 jit_solution(7045462796792222953)
XLA Ops:
  7.2 0.7 all-gather.2.cloned.1.call-update
  7.9 32.1 %all_gather.7 = f32[512,256]{1,0:T(8,128)S(1)} all-gather(f32[32,256]{1,0:T(8,128)} %param.5), channel_id=1, replica_groups=mesh['gen'=16,'train'=32] {'gen'}, dimensions={0}, use_global_device_ids=true | all-gather | bytes 557056 | tf_op jit(solution)/shard_map/all_gather | solution.py:34
  40.1 1.3 fusion.7
  41.4 1.3 fusion.6
  42.7 32.3 %all-gather.2.cloned.1.call-done = f32[1024,256]{1,0:T(8,128)} async-done(((f32[32,256]{1,0:T(8,128)}), f32[1024,256]{1,0:T(8,128)}) %all-gather.2.cloned.1.call-update) | async-done | bytes 1048592 | tf_op jit(solution)/shard_map/all_gather | solution.py:35
  75.0 1.4 multiply_reduce_fusion.1
  76.5 3.6 fusion
  80.0 62.3 %pmax.42 = f32[1024]{0:T(1024)S(1)} all-reduce(f32[1024]{0:T(1024)S(1)} %get-tuple-element.11), channel_id=1, replica_groups=mesh['gen'=16,'train'=32] {'train'}, use_global_device_ids=true, to_apply=%region_3.0 | all-reduce | flops 1024 | bytes 8192 | tf_op jit(solution)/shard_map/pmax | solution.py:22
  142.3 0.6 exponential_reduce_fusion.5
  143.0 66.8 %all-reduce = (f32[1024]{0:T(1024)S(1)}, f32[]{:T(128)}) all-reduce(f32[1024]{0:T(1024)S(1)} %exponential_multiply_fusion.2, f32[]{:T(128)} %get-tuple-element.9), channel_id=1, replica_groups=mesh['gen'=16,'train'=32] {'train'}, use_global_device_ids=true, to_apply=%region_5.0 | all-reduce | flops 1025 | bytes 8200 | tf_op jit(solution)/shard_map/psum | solution.py:23
  210.5 0.4 fusion.1
  210.9 0.6 exponential_reduce_fusion.4
  211.4 24.3 %pmax.43 = f32[512]{0:T(512)S(1)} all-reduce(f32[512]{0:T(512)S(1)} %fusion.1), channel_id=1, replica_groups=mesh['gen'=16,'train'=32] {'gen'}, use_global_device_ids=true, to_apply=%region_9.0 | all-reduce | flops 512 | bytes 4096 | tf_op jit(solution)/shard_map/pmax | solution.py:28
  235.7 22.1 %all-reduce.1 = (f32[512]{0:T(512)S(1)}, f32[]{:T(128)}) all-reduce(f32[512]{0:T(512)S(1)} %exponential_multiply_fusion.5, f32[]{:T(128)} %get-tuple-element.7), channel_id=1, replica_groups=mesh['gen'=16,'train'=32] {'gen'}, use_global_device_ids=true, to_apply=%region_11.0 | all-reduce | flops 513 | bytes 4104 | tf_op jit(solution)/shard_map/psum | solution.py:29
  258.5 0.3 fusion.2
  258.9 0.7 exponential_reduce_fusion.3
  259.5 76.6 %pmax.44 = f32[1024]{0:T(1024)S(1)} all-reduce(f32[1024]{0:T(1024)S(1)} %fusion.2), channel_id=1, replica_groups=mesh['gen'=16,'train'=32] {'train'}, use_global_device_ids=true, to_apply=%region_15.0 | all-reduce | flops 1024 | bytes 8192 | tf_op jit(solution)/shard_map/pmax | solution.py:22
  336.2 62.7 %psum.79 = f32[1024]{0:T(1024)S(1)} all-reduce(f32[1024]{0:T(1024)S(1)} %exponential_multiply_fusion.1), channel_id=1, replica_groups=mesh['gen'=16,'train'=32] {'train'}, use_global_device_ids=true, to_apply=%region_17.0 | all-reduce | flops 1024 | bytes 8192 | tf_op jit(solution)/shard_map/psum | solution.py:23
  398.9 0.4 fusion.3
  399.2 0.6 exponential_reduce_fusion.2
  399.8 21.9 %pmax.45 = f32[512]{0:T(512)S(1)} all-reduce(f32[512]{0:T(512)S(1)} %fusion.3), channel_id=1, replica_groups=mesh['gen'=16,'train'=32] {'gen'}, use_global_device_ids=true, to_apply=%region_19.0 | all-reduce | flops 512 | bytes 4096 | tf_op jit(solution)/shard_map/pmax | solution.py:28
  421.7 20.8 %psum.80 = f32[512]{0:T(512)S(1)} all-reduce(f32[512]{0:T(512)S(1)} %exponential_multiply_fusion.4), channel_id=1, replica_groups=mesh['gen'=16,'train'=32] {'gen'}, use_global_device_ids=true, to_apply=%region_21.0 | all-reduce | flops 512 | bytes 4096 | tf_op jit(solution)/shard_map/psum | solution.py:29
  442.4 0.3 fusion.4
  442.8 0.7 exponential_reduce_fusion.1
  443.5 76.8 %pmax.46 = f32[1024]{0:T(1024)S(1)} all-reduce(f32[1024]{0:T(1024)S(1)} %fusion.4), channel_id=1, replica_groups=mesh['gen'=16,'train'=32] {'train'}, use_global_device_ids=true, to_apply=%region_23.0 | all-reduce | flops 1024 | bytes 8192 | tf_op jit(solution)/shard_map/pmax | solution.py:22
  520.3 62.7 %psum.81 = f32[1024]{0:T(1024)S(1)} all-reduce(f32[1024]{0:T(1024)S(1)} %exponential_multiply_fusion), channel_id=1, replica_groups=mesh['gen'=16,'train'=32] {'train'}, use_global_device_ids=true, to_apply=%region_25.0 | all-reduce | flops 1024 | bytes 8192 | tf_op jit(solution)/shard_map/psum | solution.py:23
  583.0 0.4 fusion.5
  583.4 0.6 exponential_reduce_fusion
  583.9 21.1 %pmax.47 = f32[512]{0:T(512)S(1)} all-reduce(f32[512]{0:T(512)S(1)} %fusion.5), channel_id=1, replica_groups=mesh['gen'=16,'train'=32] {'gen'}, use_global_device_ids=true, to_apply=%region_27.0 | all-reduce | flops 512 | bytes 4096 | tf_op jit(solution)/shard_map/pmax | solution.py:28
  605.1 20.8 %psum.82 = f32[512]{0:T(512)S(1)} all-reduce(f32[512]{0:T(512)S(1)} %exponential_multiply_fusion.3), channel_id=1, replica_groups=mesh['gen'=16,'train'=32] {'gen'}, use_global_device_ids=true, to_apply=%region_29.0 | all-reduce | flops 512 | bytes 4096 | tf_op jit(solution)/shard_map/psum | solution.py:29
  625.9 1.7 multiply_reduce_fusion
  627.6 111.3 %psum.83 = f32[]{:T(128)} all-reduce(f32[]{:T(128)} %multiply_reduce_fusion), channel_id=1, replica_groups=mesh['gen'=16,'train'=32] {'gen','train'}, use_global_device_ids=true, to_apply=%region_31.0 | all-reduce | flops 1 | bytes 8 | tf_op jit(solution)/shard_map/psum | solution.py:70
  (24 shorter events, 0.3 us)
Async XLA Ops:
  7.2 67.8 %all-gather.2.cloned.1.call-start = ((), (), s32[]{:S(2)}) async-start(), calls=%async_computation | async-start | bytes 1081344 | tf_op jit(solution)/shard_map/all_gather | solution.py:35
  583.0 42.9 %copy-start = (f32[1024]{0:T(1024)}, f32[1024]{0:T(1024)S(1)}, u32[]{:S(2)}) copy-start(f32[1024]{0:T(1024)S(1)} %subtract_multiply_fusion.1) | copy-start | bytes 12292
  583.0 22.1 %copy-start.1 = (f32[1024]{0:T(1024)S(1)}, f32[1024]{0:T(1024)}, u32[]{:S(2)}) copy-start(f32[1024]{0:T(1024)} %param.6) | copy-start | bytes 12292
  583.0 22.1 %copy-start.3 = (f32[512]{0:T(512)S(1)}, f32[512]{0:T(512)}, u32[]{:S(2)}) copy-start(f32[512]{0:T(512)} %param.7) | copy-start | bytes 6148
  625.9 113.0 %copy-start.2 = (f32[512]{0:T(512)}, f32[512]{0:T(512)S(1)}, u32[]{:S(2)}) copy-start(f32[512]{0:T(512)S(1)} %subtract_multiply_fusion.4) | copy-start | bytes 6148
Sparse Core Ops, SparseCore 0:
  11.1 63.8 all-gather.1
where the time goes:
time: 746 us
  blocking collectives  682 us (91%)
  waiting for transfers between devices  33 us (4%)
  between operations  15.5 us (2%)
  other arithmetic  11.4 us (2%)
    pmax x3, blocking collectives, reduce_rows(): highest = lax.pmax(local_max, 'train')  216 us
    psum x3, blocking collectives, reduce_rows(): lax.psum((local_sum * jnp.exp(local_max - highest), local_mass), 'train')  192 us
    psum x1, blocking collectives, shards(): transport = lax.psum(local_cost, ('gen', 'train'))  111 us
    pmax x3, blocking collectives, reduce_cols(): highest = lax.pmax(local_max, 'gen')  67.3 us
    psum x3, blocking collectives, reduce_cols(): lax.psum((local_sum * jnp.exp(local_max - highest), local_mass), 'gen')  63.6 us
    all_gather x1, waiting for transfers between devices, shards(): gen_block = lax.all_gather(gen_embed, 'train', axis=0, tiled=True)  32.3 us
    all_gather x1, blocking collectives, shards(): train_block = lax.all_gather(train_embed, 'gen', axis=0, tiled=True)  32.1 us
  transfers between devices with their start and end apart: 1, of which 1 were waited for; matrix products, arithmetic and copies ran while one was open for 0% of the time, Pallas kernels for 0%

commit v1 on v0

v1 whole, which is shorter than its diff:
```python
import jax
import jax.numpy as jnp
from jax import lax
from jax.sharding import PartitionSpec as P

ITERS = 3


EPSILON = 0.05


def exchange(values, axis, count):
    copies = jnp.broadcast_to(values[None], (count,) + values.shape)
    return lax.all_to_all(copies, axis, 0, 0)


def combine(logs):
    highest = jnp.max(logs, axis=0)
    return highest + jnp.log(jnp.sum(jnp.exp(logs - highest[None]), axis=0))


def shards(n_gen, n_train, gen_embed, train_embed, row_mass, col_mass):
    width = gen_embed.shape[1]
    rows, cols = row_mass.shape[0], col_mass.shape[0]
    gen_block = exchange(gen_embed, "train", n_train).reshape(rows, width)
    train_block = exchange(train_embed, "gen", n_gen).reshape(cols, width)
    gen_sq = jnp.sum(gen_block * gen_block, axis=1)
    train_sq = jnp.sum(train_block * train_block, axis=1)
    inner = jnp.dot(
        gen_block, train_block.T, precision=lax.Precision.HIGHEST, preferred_element_type=jnp.float32
    )
    affinity = (2.0 * inner - gen_sq[:, None] - train_sq[None, :]) * (1.0 / (width * EPSILON))

    log_gen = jnp.log(row_mass)
    log_train = jnp.log(col_mass)
    gen_local = jnp.broadcast_to(jnp.sum(row_mass), (128,))
    train_local = jnp.broadcast_to(jnp.sum(col_mass), (128,))
    col_pot = jnp.zeros((cols,), jnp.float32)
    log_gen_total = log_train_total = train_total = None
    for iteration in range(ITERS):
        scores = affinity + (col_pot + log_train)[None, :]
        highest = jnp.max(scores, axis=1)
        local = highest + jnp.log(jnp.sum(jnp.exp(scores - highest[:, None]), axis=1))
        if iteration == 0:
            got = exchange(jnp.concatenate([local, train_local]), "train", n_train)
            train_total = jnp.sum(got[:, rows])
            log_train_total = jnp.log(train_total)
            got = got[:, :rows]
        else:
            got = exchange(local, "train", n_train)
        row_pot = log_train_total - combine(got)
        scores = affinity + (row_pot + log_gen)[:, None]
        highest = jnp.max(scores, axis=0)
        weights = jnp.exp(scores - highest[None, :])
        total = jnp.sum(weights, axis=0)
        local = highest + jnp.log(total)
        if iteration == 0:
            got = exchange(jnp.concatenate([local, gen_local]), "gen", n_gen)
            log_gen_total = jnp.log(jnp.sum(got[:, cols]))
            got = got[:, :cols]
        elif iteration < ITERS - 1:
            got = exchange(local, "gen", n_gen)
        else:
            mean = jnp.sum(weights * affinity, axis=0) / total
            both = exchange(jnp.stack([local, mean]), "gen", n_gen)
            got = both[:, 0]
            share = jnp.exp(got - jnp.max(got, axis=0)[None])
            mean = jnp.sum(share * both[:, 1], axis=0) / jnp.sum(share, axis=0)
        col_pot = log_gen_total - combine(got)
    local_cost = -EPSILON * jnp.sum(col_mass * mean) / train_total
    transport = jnp.sum(exchange(jnp.broadcast_to(local_cost, (128,)), "train", n_train)[:, 0])
    return (EPSILON * row_pot, EPSILON * col_pot, transport)


def solution(mesh):
    in_specs = (P(("gen", "train"), None), P(("train", "gen"), None), P("gen"), P("train"))
    out_specs = (P("gen"), P("train"), P())

    def body(*args):
        return shards(mesh.shape["gen"], mesh.shape["train"], *args)

    return jax.shard_map(body, mesh=mesh, in_specs=in_specs, out_specs=out_specs, check_vma=False)
```

time: 746 us -> 185 us (0.25)
  blocking collectives: 682 us -> 127 us
  starting transfers between devices: 0.04 us -> 13.7 us
  between operations: 15.5 us -> 3.66 us
  waiting for transfers between devices: 33 us -> 22.1 us
    psum x7 -> x0, blocking collectives: 367 us -> none  [the longest x3 192 us: reduce_rows(): lax.psum((local_sum * jnp.exp(local_max - highest), local_mass), 'train')]
    pmax x6 -> x0, blocking collectives: 283 us -> none  [the longest x3 216 us: reduce_rows(): highest = lax.pmax(local_max, 'train')]
    all_to_all x0 -> x8, blocking collectives: none -> 127 us  [exchange(): return lax.all_to_all(copies, axis, 0, 0)]
    all_gather x1 -> x0, waiting for transfers between devices: 32.3 us -> none  [shards(): gen_block = lax.all_gather(gen_embed, 'train', axis=0, tiled=True)]
    all_gather x1 -> x0, blocking collectives: 32.1 us -> none  [shards(): train_block = lax.all_gather(train_embed, 'gen', axis=0, tiled=True)]
    all_to_all x0 -> x1, waiting for transfers between devices: none -> 22.1 us  [exchange(): return lax.all_to_all(copies, axis, 0, 0)]
    all_to_all x0 -> x1, starting transfers between devices: none -> 13.7 us  [exchange(): return lax.all_to_all(copies, axis, 0, 0)]
where the time goes in v1:
time: 185 us; the launch traced here: 184 us
  blocking collectives  127 us (69%)
  waiting for transfers between devices  22.1 us (12%)
  starting transfers between devices  13.7 us (7%)
  other arithmetic  10.1 us (5%)
  local copies, waits for them, and re-layouts  4.05 us (2%)
  between operations  3.66 us (2%)
  matrix products  3.27 us (2%)
    all_to_all x8, blocking collectives, exchange(): return lax.all_to_all(copies, axis, 0, 0)  127 us
    all_to_all x1, waiting for transfers between devices, exchange(): return lax.all_to_all(copies, axis, 0, 0)  22.1 us
    all_to_all x1, starting transfers between devices, exchange(): return lax.all_to_all(copies, axis, 0, 0)  13.7 us
  transfers between devices with their start and end apart: 1, of which 1 were waited for; matrix products, arithmetic and copies ran while one was open for 0% of the time, Pallas kernels for 0%

profile of v1, /device:TPU:1, one launch (start us, length us, event | category | flops | bytes accessed | tf_op | source)
XLA Modules:
  0.0 184.3 jit_solution(6465490049000168909)
XLA Ops:
  0.6 0.9 broadcast_in_dim.16
  1.5 26.5 %all_to_all.69 = f32[32,32,256]{2,1,0:T(8,128)S(1)} all-to-all(f32[32,32,256]{2,1,0:T(8,128)S(1)} %broadcast_in_dim.16), channel_id=1, replica_groups=mesh['gen'=16,'train'=32] {'train'}, dimensions={0} | all-to-all | bytes 2097152 | tf_op jit(solution)/shard_map/all_to_all | solution.py:14
  28.1 0.8 broadcast_in_dim.17
  28.9 13.7 %all-to-all-start.1 = ((f32[16,32,256]{2,1,0:T(8,128)}), f32[16,32,256]{2,1,0:T(8,128)S(1)}, u32[]{:S(2)}, u32[]{:S(2)}) async-start(f32[16,32,256]{2,1,0:T(8,128)} %broadcast_in_dim.17), calls=%async_computation.1 | async-start | bytes 1048576 | tf_op jit(solution)/shard_map/all_to_all | solution.py:14
  42.6 0.6 fusion.13
  43.5 22.1 %all-to-all-done.1 = f32[16,32,256]{2,1,0:T(8,128)S(1)} async-done(((f32[16,32,256]{2,1,0:T(8,128)}), f32[16,32,256]{2,1,0:T(8,128)S(1)}, u32[]{:S(2)}, u32[]{:S(2)}) %all-to-all-start.1) | async-done | bytes 524320 | tf_op jit(solution)/shard_map/all_to_all | solution.py:14
  65.9 0.6 copy-done
  66.4 3.3 %add_reduce_fusion.5 = (f32[1024]{0:T(1024)S(1)}, f32[1024,512]{1,0:T(8,128)S(1)}) fusion(f32[512]{0:T(512)S(1)} %get-tuple-element.19, f32[512]{0:T(512)S(1)} %sub.151, f32[1024]{0:T(1024)S(1)} %sub.148, f32[1024,256]{1,0:T(8,128)S(1)} %bitcast.45, f32[512,256]{1,0:T(8,128)} %bitcast.46), kind=kOutput, calls=%fused_computation.14 | convolution fusion | flops 1613757440 | bytes 3682304 | tf_op jit(solution)/shard_map/dot_general | solution.py:29
  69.7 0.6 exponential_reduce_fusion.4
  70.3 0.7 concatenate.6
  71.0 18.0 %all_to_all.70 = f32[32,1,1152]{2,1,0:T(1,128)S(1)} all-to-all(f32[32,1,1152]{2,1,0:T(1,128)S(1)} %broadcast_in_dim.18), channel_id=1, replica_groups=mesh['gen'=16,'train'=32] {'train'}, dimensions={0} | all-to-all | bytes 294912 | tf_op jit(solution)/shard_map/all_to_all | solution.py:14
  89.0 0.6 slice_reduce_fusion.3
  90.4 0.6 fusion.12
  91.2 0.4 exponential_reduce_fusion.3
  91.6 0.7 concatenate.7
  92.3 17.5 %all_to_all.71 = f32[16,1,640]{2,1,0:T(1,128)S(1)} all-to-all(f32[16,1,640]{2,1,0:T(1,128)S(1)} %broadcast_in_dim.19), channel_id=1, replica_groups=mesh['gen'=16,'train'=32] {'gen'}, dimensions={0} | all-to-all | bytes 81920 | tf_op jit(solution)/shard_map/all_to_all | solution.py:14
  109.9 0.6 slice_reduce_fusion.4
  111.2 0.2 add_reduce_fusion.3
  111.5 0.6 exponential_reduce_fusion.2
  112.1 12.7 %all_to_all.72 = f32[32,1,1024]{2,1,0:T(1,128)S(1)} all-to-all(f32[32,1,1024]{2,1,0:T(1,128)S(1)} %broadcast_in_dim.20), channel_id=1, replica_groups=mesh['gen'=16,'train'=32] {'train'}, dimensions={0} | all-to-all | bytes 262144 | tf_op jit(solution)/shard_map/all_to_all | solution.py:14
  125.0 0.2 add_reduce_fusion.2
  125.2 0.4 exponential_reduce_fusion.1
  125.7 14.1 %all_to_all.73 = f32[16,1,512]{2,1,0:T(1,128)S(1)} all-to-all(f32[16,1,512]{2,1,0:T(1,128)S(1)} %broadcast_in_dim.21), channel_id=1, replica_groups=mesh['gen'=16,'train'=32] {'gen'}, dimensions={0} | all-to-all | bytes 65536 | tf_op jit(solution)/shard_map/all_to_all | solution.py:14
  139.8 0.2 add_reduce_fusion.1
  140.1 0.6 exponential_reduce_fusion
  140.7 12.3 %all_to_all.74 = f32[32,1,1024]{2,1,0:T(1,128)S(1)} all-to-all(f32[32,1,1024]{2,1,0:T(1,128)S(1)} %broadcast_in_dim.22), channel_id=1, replica_groups=mesh['gen'=16,'train'=32] {'train'}, dimensions={0} | all-to-all | bytes 262144 | tf_op jit(solution)/shard_map/all_to_all | solution.py:14
  153.2 0.6 log_add_fusion.3
  154.0 0.6 fusion
  154.7 14.3 %all_to_all.75 = f32[16,2,512]{2,1,0:T(2,128)S(1)} all-to-all(f32[16,2,512]{2,1,0:T(2,128)S(1)} %broadcast_in_dim.23), channel_id=1, replica_groups=mesh['gen'=16,'train'=32] {'gen'}, dimensions={0} | all-to-all | bytes 131072 | tf_op jit(solution)/shard_map/all_to_all | solution.py:14
  169.0 1.3 multiply_reduce_fusion.3
  171.7 12.0 %all_to_all.76 = f32[32,1,128]{2,1,0:T(1,128)S(1)} all-to-all(f32[32,1,128]{2,1,0:T(1,128)S(1)} %broadcast_in_dim_broadcast_in_dim_broadcast_in_dim.3), channel_id=1, replica_groups=mesh['gen'=16,'train'=32] {'train'}, dimensions={0} | all-to-all | bytes 32768 | tf_op jit(solution)/shard_map/all_to_all | solution.py:14
  183.7 0.6 slice_reduce_fusion.2
  (44 shorter events, 1.9 us)
Async XLA Ops:
  0.6 27.4 %copy-start.2 = (f32[32,256]{1,0:T(8,128)S(1)}, f32[32,256]{1,0:T(8,128)}, u32[]{:S(2)}) copy-start(f32[32,256]{1,0:T(8,128)} %param.5) | copy-start | bytes 98308
  1.5 41.1 %copy-start.3 = (f32[512]{0:T(512)S(1)}, f32[512]{0:T(512)}, u32[]{:S(2)}) copy-start(f32[512]{0:T(512)} %param.7) | copy-start | bytes 6148
  28.9 36.7 %all-to-all-start.1 = ((f32[16,32,256]{2,1,0:T(8,128)}), f32[16,32,256]{2,1,0:T(8,128)S(1)}, u32[]{:S(2)}, u32[]{:S(2)}) async-start(f32[16,32,256]{2,1,0:T(8,128)} %broadcast_in_dim.17), calls=%async_computation.1 | async-start | bytes 1048576 | tf_op jit(solution)/shard_map/all_to_all | solution.py:14
  65.6 0.8 copy-start
  69.7 20.7 %copy-start.1 = (f32[1024]{0:T(1024)S(1)}, f32[1024]{0:T(1024)}, u32[]{:S(2)}) copy-start(f32[1024]{0:T(1024)} %param.6) | copy-start | bytes 12292

commit v2 on v1

v2 whole, which is shorter than its diff:
```python
import jax
import jax.numpy as jnp
from jax import lax
from jax.sharding import PartitionSpec as P

ITERS = 3


EPSILON = 0.05


def exchange(values, axis, count):
    copies = jnp.broadcast_to(values[None], (count,) + values.shape)
    return lax.all_to_all(copies, axis, 0, 0)


def combine(logs):
    highest = jnp.max(logs, axis=0)
    return highest + jnp.log(jnp.sum(jnp.exp(logs - highest[None]), axis=0))


def shards(n_gen, n_train, gen_embed, train_embed, row_mass, col_mass):
    width = gen_embed.shape[1]
    rows, cols = row_mass.shape[0], col_mass.shape[0]
    gen_block = exchange(gen_embed, "train", n_train).reshape(rows, width)
    train_block = lax.all_gather(train_embed, "gen", axis=0, tiled=True)
    gen_sq = jnp.sum(gen_block * gen_block, axis=1)
    train_sq = jnp.sum(train_block * train_block, axis=1)
    inner = jnp.dot(
        gen_block, train_block.T, precision=lax.Precision.HIGHEST, preferred_element_type=jnp.float32
    )
    affinity = (2.0 * inner - gen_sq[:, None] - train_sq[None, :]) * (1.0 / (width * EPSILON))

    log_gen = jnp.log(row_mass)
    log_train = jnp.log(col_mass)
    col_pot = jnp.zeros((cols,), jnp.float32)
    for iteration in range(ITERS):
        scores = affinity + (col_pot + log_train)[None, :]
        highest = jnp.max(scores, axis=1)
        local = highest + jnp.log(jnp.sum(jnp.exp(scores - highest[:, None]), axis=1))
        row_pot = -combine(exchange(local, "train", n_train))
        scores = affinity + (row_pot + log_gen)[:, None]
        highest = jnp.max(scores, axis=0)
        weights = jnp.exp(scores - highest[None, :])
        total = jnp.sum(weights, axis=0)
        local = highest + jnp.log(total)
        if iteration < ITERS - 1:
            col_pot = -combine(exchange(local, "gen", n_gen))
    mean = jnp.sum(weights * affinity, axis=0) / total
    mass = jnp.sum(row_mass.reshape(-1, cols), axis=0)
    got = exchange(jnp.stack([local, mean, mass]), "gen", n_gen)
    logs = got[:, 0]
    highest = jnp.max(logs, axis=0)
    share = jnp.exp(logs - highest[None])
    total = jnp.sum(share, axis=0)
    col_pot = -(highest + jnp.log(total))
    mean = jnp.sum(share * got[:, 1], axis=0) / total
    log_gen_total = jnp.log(jnp.sum(got[:, 2]))
    costs = jnp.sum((col_mass * mean).reshape(-1, 128), axis=0)
    mass = jnp.sum(col_mass.reshape(-1, 128), axis=0)
    got = exchange(jnp.stack([costs, mass]), "train", n_train)
    train_total = jnp.sum(got[:, 1])
    log_train_total = jnp.log(train_total)
    transport = -EPSILON * jnp.sum(got[:, 0]) / train_total
    row_shift = ITERS * log_train_total - (ITERS - 1) * log_gen_total
    col_shift = ITERS * (log_gen_total - log_train_total)
    return (EPSILON * (row_pot + row_shift), EPSILON * (col_pot + col_shift), transport)


def solution(mesh):
    in_specs = (P(("gen", "train"), None), P(("train", "gen"), None), P("gen"), P("train"))
    out_specs = (P("gen"), P("train"), P())

    def body(*args):
        return shards(mesh.shape["gen"], mesh.shape["train"], *args)

    return jax.shard_map(body, mesh=mesh, in_specs=in_specs, out_specs=out_specs, check_vma=False)
```

time: 185 us -> 168 us (0.908)
  blocking collectives: 127 us -> 111 us
  starting transfers between devices: 13.7 us -> 21.3 us
  waiting for transfers between devices: 22.1 us -> 14.5 us
    all_to_all x8 -> x5, blocking collectives: 127 us -> 80 us  [exchange(): return lax.all_to_all(copies, axis, 0, 0)]
    all_gather x0 -> x1, blocking collectives: none -> 30.5 us  [shards(): train_block = lax.all_gather(train_embed, 'gen', axis=0, tiled=True)]
    all_to_all x1 -> x3, waiting for transfers between devices: 22.1 us -> 14.5 us  [exchange(): return lax.all_to_all(copies, axis, 0, 0)]
    all_to_all x1 -> x3, starting transfers between devices: 13.7 us -> 21.3 us  [exchange(): return lax.all_to_all(copies, axis, 0, 0)]
    reduce_sum x7 -> x6, other arithmetic: 4.31 us -> 1.96 us  [the longest x1 0.68 us: shards(): log_gen_total = jnp.log(jnp.sum(got[:, 2]))]
  transfers between devices with their start and end apart: 1 -> 3, of which waited for: 1 -> 2; matrix products, arithmetic and copies ran while one was open for 0% -> 0% of each run, Pallas kernels for 0% -> 0%
where the time goes in v2:
time: 168 us; the launch traced here: 167 us
  blocking collectives  111 us (66%)
  starting transfers between devices  21.3 us (13%)
  waiting for transfers between devices  14.5 us (9%)
  other arithmetic  8.41 us (5%)
  between operations  4.75 us (3%)
  local copies, waits for them, and re-layouts  4.35 us (3%)
  matrix products  3.27 us (2%)
    all_to_all x5, blocking collectives, exchange(): return lax.all_to_all(copies, axis, 0, 0)  80 us
    all_gather x1, blocking collectives, shards(): train_block = lax.all_gather(train_embed, 'gen', axis=0, tiled=True)  30.5 us
    all_to_all x3, starting transfers between devices, exchange(): return lax.all_to_all(copies, axis, 0, 0)  21.3 us
    all_to_all x3, waiting for transfers between devices, exchange(): return lax.all_to_all(copies, axis, 0, 0)  14.5 us
    broadcast_in_dim x8, local copies, waits for them, and re-layouts, exchange(): copies = jnp.broadcast_to(values[None], (count,) + values.shape)  3.4 us
  transfers between devices with their start and end apart: 3, of which 2 were waited for; matrix products, arithmetic and copies ran while one was open for 0% of the time, Pallas kernels for 0%

profile of v2, /device:TPU:1, one launch (start us, length us, event | category | flops | bytes accessed | tf_op | source)
XLA Modules:
  0.0 167.0 jit_solution(17910181379783282524)
XLA Ops:
  0.7 1.9 %broadcast_in_dim.16 = f32[32,32,256]{2,1,0:T(8,128)} broadcast(f32[32,256]{1,0:T(8,128)} %param.4), dimensions={1,2} | broadcast | bytes 1081344 | tf_op jit(solution)/shard_map/broadcast_in_dim | solution.py:13
  2.5 10.5 %all-to-all-start = ((f32[32,32,256]{2,1,0:T(8,128)}), f32[32,32,256]{2,1,0:T(8,128)S(1)}, u32[]{:S(2)}, u32[]{:S(2)}) async-start(f32[32,32,256]{2,1,0:T(8,128)} %broadcast_in_dim.16), calls=%async_computation | async-start | bytes 2097152 | tf_op jit(solution)/shard_map/all_to_all | solution.py:14
  13.0 30.5 %all_gather.3 = f32[512,256]{1,0:T(8,128)S(1)} all-gather(f32[32,256]{1,0:T(8,128)S(1)} %copy-done.2), channel_id=1, replica_groups=mesh['gen'=16,'train'=32] {'gen'}, dimensions={0}, use_global_device_ids=true | all-gather | bytes 557056 | tf_op jit(solution)/shard_map/all_gather | solution.py:26
  43.6 0.8 copy-done
  44.8 3.3 %add_reduce_fusion.5 = (f32[1024]{0:T(1024)S(1)}, f32[1024,512]{1,0:T(8,128)S(1)}) fusion(f32[512]{0:T(512)S(1)} %log.76, f32[512]{0:T(512)S(1)} %multiply_reduce_fusion.2, f32[1024]{0:T(1024)S(1)} %sub.120, f32[1024,256]{1,0:T(8,128)S(1)} %bitcast.58, f32[512,256]{1,0:T(8,128)} %copy-done), kind=kOutput, calls=%fused_computation.14 | convolution fusion | flops 1613757440 | bytes 3682304 | tf_op jit(solution)/shard_map/dot_general | solution.py:29
  48.1 0.6 exponential_reduce_fusion.4
  48.8 21.0 %all_to_all.60 = f32[32,1,1024]{2,1,0:T(1,128)S(1)} all-to-all(f32[32,1,1024]{2,1,0:T(1,128)S(1)} %broadcast_in_dim.17), channel_id=1, replica_groups=mesh['gen'=16,'train'=32] {'train'}, dimensions={0} | all-to-all | bytes 262144 | tf_op jit(solution)/shard_map/all_to_all | solution.py:14
  69.9 0.2 add_reduce_fusion.4
  70.1 0.4 exponential_reduce_fusion.3
  70.6 17.6 %all_to_all.61 = f32[16,1,512]{2,1,0:T(1,128)S(1)} all-to-all(f32[16,1,512]{2,1,0:T(1,128)S(1)} %broadcast_in_dim.18), channel_id=1, replica_groups=mesh['gen'=16,'train'=32] {'gen'}, dimensions={0} | all-to-all | bytes 65536 | tf_op jit(solution)/shard_map/all_to_all | solution.py:14
  88.3 0.2 add_reduce_fusion.3
  88.5 0.6 exponential_reduce_fusion.2
  89.2 12.7 %all_to_all.62 = f32[32,1,1024]{2,1,0:T(1,128)S(1)} all-to-all(f32[32,1,1024]{2,1,0:T(1,128)S(1)} %broadcast_in_dim.19), channel_id=1, replica_groups=mesh['gen'=16,'train'=32] {'train'}, dimensions={0} | all-to-all | bytes 262144 | tf_op jit(solution)/shard_map/all_to_all | solution.py:14
  102.0 0.2 add_reduce_fusion.2
  102.3 0.4 exponential_reduce_fusion.1
  102.7 14.1 %all_to_all.63 = f32[16,1,512]{2,1,0:T(1,128)S(1)} all-to-all(f32[16,1,512]{2,1,0:T(1,128)S(1)} %broadcast_in_dim.20), channel_id=1, replica_groups=mesh['gen'=16,'train'=32] {'gen'}, dimensions={0} | all-to-all | bytes 65536 | tf_op jit(solution)/shard_map/all_to_all | solution.py:14
  116.9 0.2 add_reduce_fusion.1
  117.1 0.6 exponential_reduce_fusion
  117.7 0.7 broadcast_in_dim.21
  118.4 4.9 %all-to-all-start.5 = ((f32[32,1,1024]{2,1,0:T(1,128)}), f32[32,1,1024]{2,1,0:T(1,128)S(1)}, u32[]{:S(2)}, u32[]{:S(2)}) async-start(f32[32,1,1024]{2,1,0:T(1,128)} %broadcast_in_dim.21), calls=%async_computation.5 | async-start | bytes 262144 | tf_op jit(solution)/shard_map/all_to_all | solution.py:14
  123.3 7.8 %all-to-all-done.5 = f32[32,1,1024]{2,1,0:T(1,128)S(1)} async-done(((f32[32,1,1024]{2,1,0:T(1,128)}), f32[32,1,1024]{2,1,0:T(1,128)S(1)}, u32[]{:S(2)}, u32[]{:S(2)}) %all-to-all-start.5) | async-done | bytes 131104 | tf_op jit(solution)/shard_map/all_to_all | solution.py:14
  131.3 0.2 add_reduce_fusion
  131.5 0.6 fusion
  132.1 14.6 %all_to_all.64 = f32[16,3,512]{2,1,0:T(4,128)S(1)} all-to-all(f32[16,3,512]{2,1,0:T(4,128)S(1)} %broadcast_in_dim.22), channel_id=1, replica_groups=mesh['gen'=16,'train'=32] {'gen'}, dimensions={0} | all-to-all | bytes 196608 | tf_op jit(solution)/shard_map/all_to_all | solution.py:14
  146.7 0.7 slice_reduce_fusion
  147.5 0.6 broadcast_in_dim.23
  148.1 5.9 %all-to-all-start.7 = ((f32[32,2,128]{2,1,0:T(2,128)}), f32[32,2,128]{2,1,0:T(2,128)S(1)}, u32[]{:S(2)}, u32[]{:S(2)}) async-start(f32[32,2,128]{2,1,0:T(2,128)} %broadcast_in_dim.23), calls=%async_computation.7 | async-start | bytes 65536 | tf_op jit(solution)/shard_map/all_to_all | solution.py:14
  154.7 6.7 %all-to-all-done.7 = f32[32,2,128]{2,1,0:T(2,128)S(1)} async-done(((f32[32,2,128]{2,1,0:T(2,128)}), f32[32,2,128]{2,1,0:T(2,128)S(1)}, u32[]{:S(2)}, u32[]{:S(2)}) %all-to-all-start.7) | async-done | bytes 32800 | tf_op jit(solution)/shard_map/all_to_all | solution.py:14
  161.5 0.6 reduce_sum.219
  162.1 0.6 reduce_sum.217
  164.7 0.6 add_multiply_fusion.1
  165.3 0.6 add_multiply_fusion
  (45 shorter events, 1.4 us)
Async XLA Ops:
  0.6 12.4 %copy-start.3 = (f32[512]{0:T(512)S(1)}, f32[512]{0:T(512)}, u32[]{:S(2)}) copy-start(f32[512]{0:T(512)} %param.7) | copy-start | bytes 6148
  0.6 12.4 %copy-start.2 = (f32[32,256]{1,0:T(8,128)S(1)}, f32[32,256]{1,0:T(8,128)}, u32[]{:S(2)}) copy-start(f32[32,256]{1,0:T(8,128)} %param.5) | copy-start | bytes 98308
  2.5 42.0 %all-to-all-start = ((f32[32,32,256]{2,1,0:T(8,128)}), f32[32,32,256]{2,1,0:T(8,128)S(1)}, u32[]{:S(2)}, u32[]{:S(2)}) async-start(f32[32,32,256]{2,1,0:T(8,128)} %broadcast_in_dim.16), calls=%async_computation | async-start | bytes 2097152 | tf_op jit(solution)/shard_map/all_to_all | solution.py:14
  43.6 0.8 copy-start
  48.1 21.8 %copy-start.1 = (f32[1024]{0:T(1024)S(1)}, f32[1024]{0:T(1024)}, u32[]{:S(2)}) copy-start(f32[1024]{0:T(1024)} %param.6) | copy-start | bytes 12292
  118.4 12.7 %all-to-all-start.5 = ((f32[32,1,1024]{2,1,0:T(1,128)}), f32[32,1,1024]{2,1,0:T(1,128)S(1)}, u32[]{:S(2)}, u32[]{:S(2)}) async-start(f32[32,1,1024]{2,1,0:T(1,128)} %broadcast_in_dim.21), calls=%async_computation.5 | async-start | bytes 262144 | tf_op jit(solution)/shard_map/all_to_all | solution.py:14
  148.1 13.3 %all-to-all-start.7 = ((f32[32,2,128]{2,1,0:T(2,128)}), f32[32,2,128]{2,1,0:T(2,128)S(1)}, u32[]{:S(2)}, u32[]{:S(2)}) async-start(f32[32,2,128]{2,1,0:T(2,128)} %broadcast_in_dim.23), calls=%async_computation.7 | async-start | bytes 65536 | tf_op jit(solution)/shard_map/all_to_all | solution.py:14

commit v3 on v2

v3 whole, which is shorter than its diff:
```python
import functools

import jax
import jax.numpy as jnp
from jax import lax
from jax.experimental import pallas as pl
from jax.experimental.pallas import tpu as pltpu
from jax.sharding import PartitionSpec as P

ITERS = 3


EPSILON = 0.05
LANES = 128
VMEM = pl.BlockSpec(memory_space=pltpu.VMEM)


def shape(*dims):
    return jax.ShapeDtypeStruct(dims, jnp.float32)


def call(kernel, outs, ins, scratch=(), in_specs=None, out_specs=None, limit=8 << 20):
    return pl.pallas_call(
        kernel,
        out_shape=outs,
        in_specs=in_specs or [VMEM] * len(ins),
        out_specs=out_specs or [VMEM] * len(outs),
        scratch_shapes=scratch,
        compiler_params=pltpu.CompilerParams(vmem_limit_bytes=limit),
    )(*ins)


def copies_kernel(values, out, sems):
    count = out.shape[0]
    moves = [pltpu.make_async_copy(values, out.at[k], sems.at[k]) for k in range(count)]
    for move in moves:
        move.start()
    for move in moves:
        move.wait()


def affinity_kernel(scale, gen, train, train_sq, out):
    step = 256
    for start in range(0, gen.shape[0], step):
        part = gen[start : start + step, :]
        inner = lax.dot_general(
            part,
            train[...],
            (((1,), (1,)), ((), ())),
            precision=lax.Precision.HIGHEST,
            preferred_element_type=jnp.float32,
        )
        part_sq = jnp.sum(part * part, axis=1, keepdims=True)
        out[start : start + step, :] = (2.0 * inner - part_sq - train_sq[...]) * scale


def pack_kernel(local, mean, mass, out):
    cols = local.shape[1]
    total = jnp.sum(mass[...], axis=0, keepdims=True)
    for k in range(out.shape[0]):
        out[k, :, 0:cols] = local[...]
        out[k, :, cols : 2 * cols] = mean[...]
        out[k, :, 2 * cols :] = total


def column_kernel(got, mass, col_pot, gen_mass, out):
    count, cols = got.shape[0], mass.shape[1]
    logs = [got[k, :, 0:cols] for k in range(count)]
    highest = functools.reduce(jnp.maximum, logs)
    total = weighted = jnp.zeros_like(highest)
    sums = jnp.zeros_like(gen_mass)
    for k in range(count):
        share = jnp.exp(logs[k] - highest)
        total += share
        weighted += share * got[k, :, cols : 2 * cols]
        sums += got[k, :, 2 * cols :]
    col_pot[...] = -(highest + jnp.log(total))
    gen_mass[...] = sums
    costs = mass[...] * (weighted / total)
    lanes = [slice(at, at + LANES) for at in range(0, cols, LANES)]
    cost = sum(costs[:, at] for at in lanes)
    train_mass = sum(mass[:, at] for at in lanes)
    for k in range(out.shape[0]):
        out[k, :, 0:LANES] = cost
        out[k, :, LANES:] = train_mass


def outputs_kernel(got, row_pot, col_pot, gen_mass, row_out, col_out, cost_out):
    sums = got[0]
    for k in range(1, got.shape[0]):
        sums += got[k]
    cost = jnp.sum(sums[:, 0:LANES], axis=1, keepdims=True)
    train_total = jnp.sum(sums[:, LANES:], axis=1, keepdims=True)
    log_train = jnp.log(train_total)
    log_gen = jnp.log(jnp.sum(gen_mass[...], axis=1, keepdims=True))
    row_out[...] = EPSILON * (row_pot[...] + (ITERS * log_train - (ITERS - 1) * log_gen))
    col_out[...] = EPSILON * (col_pot[...] + ITERS * (log_gen - log_train))
    cost_out[...] = -EPSILON * cost / train_total


def exchange(values, axis, count):
    copies = jnp.broadcast_to(values[None], (count,) + values.shape)
    return lax.all_to_all(copies, axis, 0, 0)


def combine(logs):
    highest = jnp.max(logs, axis=0)
    return highest + jnp.log(jnp.sum(jnp.exp(logs - highest[None]), axis=0))


def shards(n_gen, n_train, gen_embed, train_embed, row_mass, col_mass):
    width = gen_embed.shape[1]
    rows, cols = row_mass.shape[0], col_mass.shape[0]
    (copies,) = call(
        copies_kernel,
        [shape(n_train, *gen_embed.shape)],
        [gen_embed],
        scratch=[pltpu.SemaphoreType.DMA((n_train,))],
        out_specs=[pl.BlockSpec(memory_space=pl.ANY)],
        limit=1 << 20,
    )
    gen_block = lax.all_to_all(copies, "train", 0, 0).reshape(rows, width)
    train_block = lax.all_gather(train_embed, "gen", axis=0, tiled=True)
    train_sq = jnp.sum(train_block * train_block, axis=1)
    (affinity,) = call(
        functools.partial(affinity_kernel, 1.0 / (width * EPSILON)),
        [shape(rows, cols)],
        [gen_block, train_block, train_sq[None]],
    )

    log_gen = jnp.log(row_mass)
    log_train = jnp.log(col_mass)
    col_pot = jnp.zeros((cols,), jnp.float32)
    for iteration in range(ITERS):
        scores = affinity + (col_pot + log_train)[None, :]
        highest = jnp.max(scores, axis=1)
        local = highest + jnp.log(jnp.sum(jnp.exp(scores - highest[:, None]), axis=1))
        row_pot = -combine(exchange(local, "train", n_train))
        scores = affinity + (row_pot + log_gen)[:, None]
        highest = jnp.max(scores, axis=0)
        weights = jnp.exp(scores - highest[None, :])
        total = jnp.sum(weights, axis=0)
        local = highest + jnp.log(total)
        if iteration < ITERS - 1:
            col_pot = -combine(exchange(local, "gen", n_gen))
    mean = jnp.sum(weights * affinity, axis=0) / total
    small = 1 << 20
    (packed,) = call(
        pack_kernel,
        [shape(n_gen, 1, 2 * cols + LANES)],
        [local[None], mean[None], row_mass.reshape(-1, LANES)],
        limit=small,
    )
    got = lax.all_to_all(packed, "gen", 0, 0)
    col_pot, gen_mass, packed = call(
        column_kernel,
        [shape(1, cols), shape(1, LANES), shape(n_train, 1, 2 * LANES)],
        [got, col_mass[None]],
        limit=small,
    )
    got = lax.all_to_all(packed, "train", 0, 0)
    row_out, col_out, cost = call(
        outputs_kernel,
        [shape(rows // LANES, LANES), shape(1, cols), shape(1, 1)],
        [got, row_pot.reshape(-1, LANES), col_pot, gen_mass],
        limit=small,
    )
    return (row_out.reshape(rows), col_out.reshape(cols), cost.reshape(()))


def solution(mesh):
    in_specs = (P(("gen", "train"), None), P(("train", "gen"), None), P("gen"), P("train"))
    out_specs = (P("gen"), P("train"), P())

    def body(*args):
        return shards(mesh.shape["gen"], mesh.shape["train"], *args)

    return jax.shard_map(body, mesh=mesh, in_specs=in_specs, out_specs=out_specs, check_vma=False)
```

time: 168 us -> 159 us (0.946)
  blocking collectives: 111 us -> 135 us
  waiting for transfers between devices: 14.5 us -> 0.01 us
  starting transfers between devices: 21.3 us -> 10.5 us
  Pallas kernels: 0 us -> 4.01 us
  between operations: 4.75 us -> 0.89 us
  matrix products: 3.27 us -> 0 us
  other arithmetic: 8.41 us -> 5.25 us
    all_to_all x0 -> x2, blocking collectives: none -> 26.8 us  [the longest x1 14.3 us: shards(): got = lax.all_to_all(packed, 'gen', 0, 0)]
    all_to_all x3 -> x1, waiting for transfers between devices: 14.5 us -> 0.01 us  [shards(): gen_block = lax.all_to_all(copies, 'train', 0, 0).reshape(rows, width)]
    all_to_all x3 -> x1, starting transfers between devices: 21.3 us -> 10.5 us  [shards(): gen_block = lax.all_to_all(copies, 'train', 0, 0).reshape(rows, width)]
    pallas_call x0 -> x5, Pallas kernels: none -> 4.01 us  [call(): pl.pallas_call(kernel, out_shape=outs, in_specs=in_specs or [VMEM] * len(...]
    dot_general x1 -> x0, matrix products: 3.27 us -> none  [shards(): jnp.dot(gen_block, train_block.T, precision=lax.Precision.HIGHEST, prefer...]
    broadcast_in_dim x8 -> x5, local copies, waits for them, and re-layouts: 3.4 us -> 0.26 us  [exchange(): copies = jnp.broadcast_to(values[None], (count,) + values.shape)]
    all_to_all x5, blocking collectives: 80 us -> 77.7 us  [exchange(): return lax.all_to_all(copies, axis, 0, 0)]
    unnamed x8 -> x12, local copies, waits for them, and re-layouts: 0.83 us -> 2.97 us
  transfers between devices with their start and end apart: 3 -> 1, of which waited for: 2 -> 0; matrix products, arithmetic and copies ran while one was open for 0% -> 0% of each run, Pallas kernels for 0% -> 0%
where the time goes in v3:
time: 159 us
  blocking collectives  135 us (85%)
  starting transfers between devices  10.5 us (7%)
  other arithmetic  5.25 us (3%)
  Pallas kernels  4.01 us (3%)
  local copies, waits for them, and re-layouts  3.23 us (2%)
    all_to_all x5, blocking collectives, exchange(): return lax.all_to_all(copies, axis, 0, 0)  77.7 us
    all_gather x1, blocking collectives, shards(): train_block = lax.all_gather(train_embed, 'gen', axis=0, tiled=True)  30.5 us
    all_to_all x1, blocking collectives, shards(): got = lax.all_to_all(packed, 'gen', 0, 0)  14.3 us
    all_to_all x1, blocking collectives, shards(): got = lax.all_to_all(packed, 'train', 0, 0)  12.5 us
    all_to_all x1, starting transfers between devices, shards(): gen_block = lax.all_to_all(copies, 'train', 0, 0).reshape(rows, width)  10.5 us
    pallas_call x5, Pallas kernels, call(): pl.pallas_call(kernel, out_shape=outs, in_specs=in_specs or [VMEM] * len(...  4.01 us
  transfers between devices with their start and end apart: 1, of which 0 were waited for; matrix products, arithmetic and copies ran while one was open for 0% of the time, Pallas kernels for 0%

profile of v3, /device:TPU:1, one launch (start us, length us, event | category | flops | bytes accessed | tf_op | source)
XLA Modules:
  0.0 158.9 jit_solution(5656994806408066240)
XLA Ops:
  0.6 0.7 copy-done.3
  1.4 1.3 shard_map.67
  2.7 10.5 %all-to-all-start = ((f32[32,32,256]{2,1,0:T(8,128)}), f32[32,32,256]{2,1,0:T(8,128)S(1)}, u32[]{:S(2)}, u32[]{:S(2)}) async-start(f32[32,32,256]{2,1,0:T(8,128)} %shard_map.67), calls=%async_computation | async-start | bytes 2097152 | tf_op jit(solution)/shard_map/all_to_all | solution.py:122
  13.2 30.5 %all_gather.3.train = f32[512,256]{1,0:T(8,128)S(1)} all-gather(f32[32,256]{1,0:T(8,128)S(1)} %copy-done.5), channel_id=1, replica_groups=mesh['gen'=16,'train'=32] {'gen'}, dimensions={0}, use_global_device_ids=true | all-gather | bytes 557056 | tf_op jit(solution)/shard_map/all_gather | solution.py:123
  43.7 0.1 multiply_reduce_fusion.1
  43.9 1.0 copy-done
  44.9 1.2 copy-done.1
  46.1 1.9 %shard_map.68 = f32[1024,512]{1,0:T(8,128)S(1)} custom-call(f32[1024,256]{1,0:T(8,128)S(1)} %bitcast.41, f32[512,256]{1,0:T(8,128)S(1)} %all_gather.3.train, f32[1,512]{1,0:T(1,128)S(1)} %bitcast.44), custom_call_target="tpu_custom_call" | custom-call | tf_op jit(solution)/shard_map/pallas_call | solution.py:23
  48.1 0.2 add_reduce_fusion.5
  48.3 0.6 exponential_reduce_fusion.4
  48.9 21.0 %all_to_all.60 = f32[32,1,1024]{2,1,0:T(1,128)S(1)} all-to-all(f32[32,1,1024]{2,1,0:T(1,128)S(1)} %broadcast_in_dim.15), channel_id=1, replica_groups=mesh['gen'=16,'train'=32] {'train'}, dimensions={0} | all-to-all | bytes 262144 | tf_op jit(solution)/shard_map/all_to_all | solution.py:103
  69.9 0.1 reduce_max.100
  70.1 0.2 add_reduce_fusion.4
  70.3 0.4 exponential_reduce_fusion.3
  70.8 17.6 %all_to_all.61 = f32[16,1,512]{2,1,0:T(1,128)S(1)} all-to-all(f32[16,1,512]{2,1,0:T(1,128)S(1)} %broadcast_in_dim.16), channel_id=1, replica_groups=mesh['gen'=16,'train'=32] {'gen'}, dimensions={0} | all-to-all | bytes 65536 | tf_op jit(solution)/shard_map/all_to_all | solution.py:103
  88.5 0.2 add_reduce_fusion.3
  88.7 0.6 exponential_reduce_fusion.2
  89.3 12.7 %all_to_all.62 = f32[32,1,1024]{2,1,0:T(1,128)S(1)} all-to-all(f32[32,1,1024]{2,1,0:T(1,128)S(1)} %broadcast_in_dim.17), channel_id=1, replica_groups=mesh['gen'=16,'train'=32] {'train'}, dimensions={0} | all-to-all | bytes 262144 | tf_op jit(solution)/shard_map/all_to_all | solution.py:103
  102.0 0.1 reduce_max.104
  102.2 0.2 add_reduce_fusion.2
  102.4 0.4 exponential_reduce_fusion.1
  102.9 14.1 %all_to_all.63 = f32[16,1,512]{2,1,0:T(1,128)S(1)} all-to-all(f32[16,1,512]{2,1,0:T(1,128)S(1)} %broadcast_in_dim.18), channel_id=1, replica_groups=mesh['gen'=16,'train'=32] {'gen'}, dimensions={0} | all-to-all | bytes 65536 | tf_op jit(solution)/shard_map/all_to_all | solution.py:103
  117.1 0.2 add_reduce_fusion.1
  117.3 0.6 exponential_reduce_fusion
  117.9 0.1 broadcast_in_dim.19
  117.9 12.3 %all_to_all.64 = f32[32,1,1024]{2,1,0:T(1,128)S(1)} all-to-all(f32[32,1,1024]{2,1,0:T(1,128)S(1)} %broadcast_in_dim.19), channel_id=1, replica_groups=mesh['gen'=16,'train'=32] {'train'}, dimensions={0} | all-to-all | bytes 262144 | tf_op jit(solution)/shard_map/all_to_all | solution.py:103
  130.3 0.1 reduce_max.108
  130.4 0.2 add_reduce_fusion
  130.7 0.6 multiply_reduce_fusion
  131.3 14.3 %all_to_all.65.got = f32[16,1,1152]{2,1,0:T(1,128)S(1)} all-to-all(f32[16,1,1152]{2,1,0:T(1,128)S(1)} %shard_map.69), channel_id=1, replica_groups=mesh['gen'=16,'train'=32] {'gen'}, dimensions={0} | all-to-all | bytes 147456 | tf_op jit(solution)/shard_map/all_to_all | solution.py:154
  145.6 12.5 %all_to_all.66.got = f32[32,1,256]{2,1,0:T(1,128)S(1)} all-to-all(f32[32,1,256]{2,1,0:T(1,128)S(1)} %get-tuple-element.9), channel_id=1, replica_groups=mesh['gen'=16,'train'=32] {'train'}, dimensions={0} | all-to-all | bytes 65536 | tf_op jit(solution)/shard_map/all_to_all | solution.py:161
  158.1 0.7 shard_map.71
  (35 shorter events, 0.7 us)
Async XLA Ops:
  0.6 0.8 copy-start.3
  1.4 11.8 %copy-start.4 = (f32[512]{0:T(512)S(1)}, f32[512]{0:T(512)}, u32[]{:S(2)}) copy-start(f32[512]{0:T(512)} %param.7) | copy-start | bytes 6148
  1.4 11.8 %copy-start.5 = (f32[32,256]{1,0:T(8,128)S(1)}, f32[32,256]{1,0:T(8,128)}, u32[]{:S(2)}) copy-start(f32[32,256]{1,0:T(8,128)} %param.5) | copy-start | bytes 98308
  2.7 41.2 %all-to-all-start = ((f32[32,32,256]{2,1,0:T(8,128)}), f32[32,32,256]{2,1,0:T(8,128)S(1)}, u32[]{:S(2)}, u32[]{:S(2)}) async-start(f32[32,32,256]{2,1,0:T(8,128)} %shard_map.67), calls=%async_computation | async-start | bytes 2097152 | tf_op jit(solution)/shard_map/all_to_all | solution.py:122
  43.9 1.0 copy-start
  44.9 1.2 copy-start.1
  48.0 22.0 %copy-start.2 = (f32[1024]{0:T(1024)S(1)}, f32[1024]{0:T(1024)}, u32[]{:S(2)}) copy-start(f32[1024]{0:T(1024)} %param.6) | copy-start | bytes 12292

commit v4 on v3

--- a/solution.py
+++ b/solution.py
@@ -19,39 +19,29 @@
     return jax.ShapeDtypeStruct(dims, jnp.float32)
 
 
-def call(kernel, outs, ins, scratch=(), in_specs=None, out_specs=None, limit=8 << 20):
+def call(kernel, outs, ins, limit=8 << 20):
     return pl.pallas_call(
         kernel,
         out_shape=outs,
-        in_specs=in_specs or [VMEM] * len(ins),
-        out_specs=out_specs or [VMEM] * len(outs),
-        scratch_shapes=scratch,
+        in_specs=[VMEM] * len(ins),
+        out_specs=[VMEM] * len(outs),
         compiler_params=pltpu.CompilerParams(vmem_limit_bytes=limit),
     )(*ins)
 
 
-def copies_kernel(values, out, sems):
-    count = out.shape[0]
-    moves = [pltpu.make_async_copy(values, out.at[k], sems.at[k]) for k in range(count)]
-    for move in moves:
-        move.start()
-    for move in moves:
-        move.wait()
-
-
-def affinity_kernel(scale, gen, train, train_sq, out):
+def affinity_kernel(scale, twice_gen, train, train_sq, out):
     step = 256
-    for start in range(0, gen.shape[0], step):
-        part = gen[start : start + step, :]
-        inner = lax.dot_general(
+    for start in range(0, twice_gen.shape[0], step):
+        part = twice_gen[start : start + step, :]
+        twice_inner = lax.dot_general(
             part,
             train[...],
             (((1,), (1,)), ((), ())),
             precision=lax.Precision.HIGHEST,
             preferred_element_type=jnp.float32,
         )
-        part_sq = jnp.sum(part * part, axis=1, keepdims=True)
-        out[start : start + step, :] = (2.0 * inner - part_sq - train_sq[...]) * scale
+        part_sq = 0.25 * jnp.sum(part * part, axis=1, keepdims=True)
+        out[start : start + step, :] = (twice_inner - part_sq - train_sq[...]) * scale
 
 
 def pack_kernel(local, mean, mass, out):
@@ -111,21 +101,13 @@
 def shards(n_gen, n_train, gen_embed, train_embed, row_mass, col_mass):
     width = gen_embed.shape[1]
     rows, cols = row_mass.shape[0], col_mass.shape[0]
-    (copies,) = call(
-        copies_kernel,
-        [shape(n_train, *gen_embed.shape)],
-        [gen_embed],
-        scratch=[pltpu.SemaphoreType.DMA((n_train,))],
-        out_specs=[pl.BlockSpec(memory_space=pl.ANY)],
-        limit=1 << 20,
-    )
-    gen_block = lax.all_to_all(copies, "train", 0, 0).reshape(rows, width)
+    gen_block = exchange(gen_embed, "train", n_train).reshape(rows, width)
     train_block = lax.all_gather(train_embed, "gen", axis=0, tiled=True)
     train_sq = jnp.sum(train_block * train_block, axis=1)
     (affinity,) = call(
         functools.partial(affinity_kernel, 1.0 / (width * EPSILON)),
         [shape(rows, cols)],
-        [gen_block, train_block, train_sq[None]],
+        [2.0 * gen_block, train_block, train_sq[None]],
     )
 
     log_gen = jnp.log(row_mass)

time: 159 us -> 157 us (0.987)
    unnamed x12 -> x6, local copies, waits for them, and re-layouts: 2.97 us -> 0.01 us
    broadcast_in_dim x5 -> x6, local copies, waits for them, and re-layouts: 0.26 us -> 2.13 us  [exchange(): copies = jnp.broadcast_to(values[None], (count,) + values.shape)]
    pallas_call x5 -> x4, Pallas kernels: 4.01 us -> 2.76 us  [call(): pl.pallas_call(kernel, out_shape=outs, in_specs=[VMEM] * len(ins), out_sp...]
where the time goes in v4:
time: 157 us
  blocking collectives  135 us (86%)
  starting transfers between devices  10.5 us (7%)
  other arithmetic  5.33 us (3%)
  Pallas kernels  2.76 us (2%)
  local copies, waits for them, and re-layouts  2.15 us (1%)
    all_to_all x5, blocking collectives, exchange(): return lax.all_to_all(copies, axis, 0, 0)  77.7 us
    all_gather x1, blocking collectives, shards(): train_block = lax.all_gather(train_embed, 'gen', axis=0, tiled=True)  30.5 us
    all_to_all x1, blocking collectives, shards(): got = lax.all_to_all(packed, 'gen', 0, 0)  14.3 us
    all_to_all x1, blocking collectives, shards(): got = lax.all_to_all(packed, 'train', 0, 0)  12.5 us
    all_to_all x1, starting transfers between devices, exchange(): return lax.all_to_all(copies, axis, 0, 0)  10.5 us
  transfers between devices with their start and end apart: 1, of which 0 were waited for; matrix products, arithmetic and copies ran while one was open for 0% of the time, Pallas kernels for 0%

profile of v4, /device:TPU:1, one launch (start us, length us, event | category | flops | bytes accessed | tf_op | source)
XLA Modules:
  0.0 156.6 jit_solution(12608147262040519427)
XLA Ops:
  0.7 1.9 %broadcast_in_dim.16 = f32[32,32,256]{2,1,0:T(8,128)} broadcast(f32[32,256]{1,0:T(8,128)} %param.4), dimensions={1,2} | broadcast | bytes 1081344 | tf_op jit(solution)/shard_map/broadcast_in_dim | solution.py:92
  2.5 10.5 %all-to-all-start = ((f32[32,32,256]{2,1,0:T(8,128)}), f32[32,32,256]{2,1,0:T(8,128)S(1)}, u32[]{:S(2)}, u32[]{:S(2)}) async-start(f32[32,32,256]{2,1,0:T(8,128)} %broadcast_in_dim.16), calls=%async_computation | async-start | bytes 2097152 | tf_op jit(solution)/shard_map/all_to_all | solution.py:93
  13.0 30.5 %all_gather.3.train = f32[512,256]{1,0:T(8,128)S(1)} all-gather(f32[32,256]{1,0:T(8,128)S(1)} %copy-done.2), channel_id=1, replica_groups=mesh['gen'=16,'train'=32] {'gen'}, dimensions={0}, use_global_device_ids=true | all-gather | bytes 557056 | tf_op jit(solution)/shard_map/all_gather | solution.py:105
  43.6 0.1 multiply_reduce_fusion.1
  43.7 0.1 broadcast_multiply_fusion
  43.8 2.0 %shard_map.67 = f32[1024,512]{1,0:T(8,128)S(1)} custom-call(f32[1024,256]{1,0:T(8,128)S(1)} %bitcast.41, f32[512,256]{1,0:T(8,128)S(1)} %all_gather.3.train, f32[1,512]{1,0:T(1,128)S(1)} %bitcast.44), custom_call_target="tpu_custom_call" | custom-call | tf_op jit(solution)/shard_map/pallas_call | solution.py:23
  45.8 0.2 add_reduce_fusion.5
  46.0 0.6 exponential_reduce_fusion.4
  46.6 0.1 broadcast_in_dim.18
  46.7 21.0 %all_to_all.60 = f32[32,1,1024]{2,1,0:T(1,128)S(1)} all-to-all(f32[32,1,1024]{2,1,0:T(1,128)S(1)} %broadcast_in_dim.18), channel_id=1, replica_groups=mesh['gen'=16,'train'=32] {'train'}, dimensions={0} | all-to-all | bytes 262144 | tf_op jit(solution)/shard_map/all_to_all | solution.py:93
  67.6 0.1 reduce_max.100
  67.8 0.2 add_reduce_fusion.4
  68.0 0.4 exponential_reduce_fusion.3
  68.5 17.6 %all_to_all.61 = f32[16,1,512]{2,1,0:T(1,128)S(1)} all-to-all(f32[16,1,512]{2,1,0:T(1,128)S(1)} %broadcast_in_dim.19), channel_id=1, replica_groups=mesh['gen'=16,'train'=32] {'gen'}, dimensions={0} | all-to-all | bytes 65536 | tf_op jit(solution)/shard_map/all_to_all | solution.py:93
  86.2 0.2 add_reduce_fusion.3
  86.4 0.6 exponential_reduce_fusion.2
  87.0 0.1 broadcast_in_dim.20
  87.1 12.7 %all_to_all.62 = f32[32,1,1024]{2,1,0:T(1,128)S(1)} all-to-all(f32[32,1,1024]{2,1,0:T(1,128)S(1)} %broadcast_in_dim.20), channel_id=1, replica_groups=mesh['gen'=16,'train'=32] {'train'}, dimensions={0} | all-to-all | bytes 262144 | tf_op jit(solution)/shard_map/all_to_all | solution.py:93
  99.8 0.1 reduce_max.104
  99.9 0.2 add_reduce_fusion.2
  100.2 0.4 exponential_reduce_fusion.1
  100.6 14.1 %all_to_all.63 = f32[16,1,512]{2,1,0:T(1,128)S(1)} all-to-all(f32[16,1,512]{2,1,0:T(1,128)S(1)} %broadcast_in_dim.21), channel_id=1, replica_groups=mesh['gen'=16,'train'=32] {'gen'}, dimensions={0} | all-to-all | bytes 65536 | tf_op jit(solution)/shard_map/all_to_all | solution.py:93
  114.8 0.2 add_reduce_fusion.1
  115.0 0.6 exponential_reduce_fusion
  115.6 0.1 broadcast_in_dim.22
  115.7 12.3 %all_to_all.64 = f32[32,1,1024]{2,1,0:T(1,128)S(1)} all-to-all(f32[32,1,1024]{2,1,0:T(1,128)S(1)} %broadcast_in_dim.22), channel_id=1, replica_groups=mesh['gen'=16,'train'=32] {'train'}, dimensions={0} | all-to-all | bytes 262144 | tf_op jit(solution)/shard_map/all_to_all | solution.py:93
  128.0 0.1 reduce_max.108
  128.2 0.2 add_reduce_fusion
  128.4 0.6 multiply_reduce_fusion
  129.0 14.3 %all_to_all.65.got = f32[16,1,1152]{2,1,0:T(1,128)S(1)} all-to-all(f32[16,1,1152]{2,1,0:T(1,128)S(1)} %shard_map.68), channel_id=1, replica_groups=mesh['gen'=16,'train'=32] {'gen'}, dimensions={0} | all-to-all | bytes 147456 | tf_op jit(solution)/shard_map/all_to_all | solution.py:136
  143.3 12.5 %all_to_all.66.got = f32[32,1,256]{2,1,0:T(1,128)S(1)} all-to-all(f32[32,1,256]{2,1,0:T(1,128)S(1)} %get-tuple-element.9), channel_id=1, replica_groups=mesh['gen'=16,'train'=32] {'train'}, dimensions={0} | all-to-all | bytes 65536 | tf_op jit(solution)/shard_map/all_to_all | solution.py:143
  155.9 0.7 shard_map.70
  (30 shorter events, 0.5 us)
Async XLA Ops:
  0.6 12.4 %copy-start.1 = (f32[512]{0:T(512)S(1)}, f32[512]{0:T(512)}, u32[]{:S(2)}) copy-start(f32[512]{0:T(512)} %param.7) | copy-start | bytes 6148
  0.6 12.4 %copy-start.2 = (f32[32,256]{1,0:T(8,128)S(1)}, f32[32,256]{1,0:T(8,128)}, u32[]{:S(2)}) copy-start(f32[32,256]{1,0:T(8,128)} %param.5) | copy-start | bytes 98308
  2.5 41.2 %all-to-all-start = ((f32[32,32,256]{2,1,0:T(8,128)}), f32[32,32,256]{2,1,0:T(8,128)S(1)}, u32[]{:S(2)}, u32[]{:S(2)}) async-start(f32[32,32,256]{2,1,0:T(8,128)} %broadcast_in_dim.16), calls=%async_computation | async-start | bytes 2097152 | tf_op jit(solution)/shard_map/all_to_all | solution.py:93
  45.8 22.0 %copy-start = (f32[1024]{0:T(1024)S(1)}, f32[1024]{0:T(1024)}, u32[]{:S(2)}) copy-start(f32[1024]{0:T(1024)} %param.6) | copy-start | bytes 12292

commit v5 on v4

--- a/solution.py
+++ b/solution.py
@@ -13,26 +13,71 @@
 EPSILON = 0.05
 LANES = 128
 VMEM = pl.BlockSpec(memory_space=pltpu.VMEM)
+ANY = pl.BlockSpec(memory_space=pl.ANY)
 
 
 def shape(*dims):
     return jax.ShapeDtypeStruct(dims, jnp.float32)
 
 
-def call(kernel, outs, ins, limit=8 << 20):
+def call(kernel, outs, ins, scratch=(), in_specs=None, out_specs=None, limit=8 << 20):
     return pl.pallas_call(
         kernel,
         out_shape=outs,
-        in_specs=[VMEM] * len(ins),
-        out_specs=[VMEM] * len(outs),
+        in_specs=in_specs or [VMEM] * len(ins),
+        out_specs=out_specs or [VMEM] * len(outs),
+        scratch_shapes=scratch,
         compiler_params=pltpu.CompilerParams(vmem_limit_bytes=limit),
     )(*ins)
 
 
-def affinity_kernel(scale, twice_gen, train, train_sq, out):
-    step = 256
-    for start in range(0, twice_gen.shape[0], step):
-        part = twice_gen[start : start + step, :]
+def own(shape):
+    column = lax.broadcasted_iota(jnp.int32, shape, len(shape) - 1)
+    share = shape[-1] // lax.axis_size("gen")
+    return (column // share) % 2 == lax.axis_index("gen") % 2
+
+
+def partner():
+    at = lax.axis_index("train")
+    return at + 1 - 2 * (at % 2)
+
+
+def copies_kernel(values, mass, out, rows, row_mass, block, in_sems, sems):
+    many, height, width = block.shape
+    share, cols = rows.shape[0], row_mass.shape[1]
+    fetches = [
+        pltpu.make_async_copy(values, rows, in_sems.at[0]),
+        pltpu.make_async_copy(mass, row_mass, in_sems.at[1]),
+    ]
+    for fetch in fetches:
+        fetch.start()
+    for fetch in fetches:
+        fetch.wait()
+    masses = jnp.concatenate([row_mass[:, at : at + width] for at in range(0, cols, width)], axis=0)
+    rest = jnp.zeros((height - share - cols // width, width), jnp.float32)
+    whole = jnp.concatenate([rows[...], masses, rest], axis=0)
+    for k in range(many):
+        block[k] = whole
+    moves = [
+        pltpu.make_async_copy(block, out.at[pl.ds(k * many, many)], sems.at[k]) for k in range(out.shape[0] // many)
+    ]
+    for move in moves:
+        move.start()
+    for move in moves:
+        move.wait()
+
+
+def affinity_kernel(scale, twice, train, train_sq, mass, out, tile_mass, log_mass):
+    members, _, width = twice.shape
+    share = out.shape[0] // members
+    other = twice[partner(), share : share + mass.shape[1] // width, :]
+    other = 0.5 * jnp.concatenate([other[k : k + 1] for k in range(other.shape[0])], axis=1)
+    masses = jnp.where(own(mass.shape), mass[...], other)
+    tile_mass[...] = masses
+    log_mass[...] = jnp.log(masses)
+    step = 8
+    for start in range(0, members, step):
+        part = twice[start : start + step, 0:share, :].reshape(step * share, width)
         twice_inner = lax.dot_general(
             part,
             train[...],
@@ -41,7 +86,7 @@
             preferred_element_type=jnp.float32,
         )
         part_sq = 0.25 * jnp.sum(part * part, axis=1, keepdims=True)
-        out[start : start + step, :] = (twice_inner - part_sq - train_sq[...]) * scale
+        out[start * share : (start + step) * share, :] = (twice_inner - part_sq - train_sq[...]) * scale
 
 
 def pack_kernel(local, mean, mass, out):
@@ -64,7 +109,8 @@
         total += share
         weighted += share * got[k, :, cols : 2 * cols]
         sums += got[k, :, 2 * cols :]
-    col_pot[...] = -(highest + jnp.log(total))
+    potential = -(highest + jnp.log(total))
+    col_pot[...] = potential
     gen_mass[...] = sums
     costs = mass[...] * (weighted / total)
     lanes = [slice(at, at + LANES) for at in range(0, cols, LANES)]
@@ -72,25 +118,26 @@
     train_mass = sum(mass[:, at] for at in lanes)
     for k in range(out.shape[0]):
         out[k, :, 0:LANES] = cost
-        out[k, :, LANES:] = train_mass
+        out[k, :, LANES : 2 * LANES] = train_mass
+        out[k, :, 2 * LANES :] = potential
 
 
 def outputs_kernel(got, row_pot, col_pot, gen_mass, row_out, col_out, cost_out):
-    sums = got[0]
-    for k in range(1, got.shape[0]):
-        sums += got[k]
+    terms = [got[k, :, 0 : 2 * LANES] + got[k + 1, :, 0 : 2 * LANES] for k in range(0, got.shape[0], 2)]
+    sums = functools.reduce(jnp.add, terms)
     cost = jnp.sum(sums[:, 0:LANES], axis=1, keepdims=True)
     train_total = jnp.sum(sums[:, LANES:], axis=1, keepdims=True)
+    columns = jnp.where(own(col_pot.shape), col_pot[...], got[partner(), :, 2 * LANES :])
     log_train = jnp.log(train_total)
     log_gen = jnp.log(jnp.sum(gen_mass[...], axis=1, keepdims=True))
     row_out[...] = EPSILON * (row_pot[...] + (ITERS * log_train - (ITERS - 1) * log_gen))
-    col_out[...] = EPSILON * (col_pot[...] + ITERS * (log_gen - log_train))
+    col_out[...] = EPSILON * (columns + ITERS * (log_gen - log_train))
     cost_out[...] = -EPSILON * cost / train_total
 
 
-def exchange(values, axis, count):
+def exchange(values, axis, count, groups=None):
     copies = jnp.broadcast_to(values[None], (count,) + values.shape)
-    return lax.all_to_all(copies, axis, 0, 0)
+    return lax.all_to_all(copies, axis, 0, 0, axis_index_groups=groups)
 
 
 def combine(logs):
@@ -101,17 +148,41 @@
 def shards(n_gen, n_train, gen_embed, train_embed, row_mass, col_mass):
     width = gen_embed.shape[1]
     rows, cols = row_mass.shape[0], col_mass.shape[0]
-    gen_block = exchange(gen_embed, "train", n_train).reshape(rows, width)
-    train_block = lax.all_gather(train_embed, "gen", axis=0, tiled=True)
+    both = ("gen", "train")
+    groups = [
+        [g * n_train + first + (g + shift) % 2 for g in range(n_gen)]
+        for first in range(0, n_train, 2)
+        for shift in range(2)
+    ]
+    small = 1 << 20
+    height = gen_embed.shape[0] + 8
+    many = 4
+    (packed,) = call(
+        copies_kernel,
+        [shape(n_train, height, width)],
+        [gen_embed, col_mass[None]],
+        scratch=[
+            pltpu.VMEM(gen_embed.shape, jnp.float32),
+            pltpu.VMEM((1, cols), jnp.float32),
+            pltpu.VMEM((many, height, width), jnp.float32),
+            pltpu.SemaphoreType.DMA((2,)),
+            pltpu.SemaphoreType.DMA((n_train // many,)),
+        ],
+        in_specs=[ANY, ANY],
+        out_specs=[ANY],
+        limit=60 << 20,
+    )
+    twice = 2.0 * lax.all_to_all(packed, "train", 0, 0)
+    train_block = lax.all_gather(train_embed, both, axis=0, tiled=True, axis_index_groups=groups)
     train_sq = jnp.sum(train_block * train_block, axis=1)
-    (affinity,) = call(
+    affinity, tile_mass, log_train = call(
         functools.partial(affinity_kernel, 1.0 / (width * EPSILON)),
-        [shape(rows, cols)],
-        [2.0 * gen_block, train_block, train_sq[None]],
-    )
+        [shape(rows, cols), shape(1, cols), shape(1, cols)],
+        [twice, train_block, train_sq[None], col_mass[None]],
+    )
+    log_train = log_train[0]
 
     log_gen = jnp.log(row_mass)
-    log_train = jnp.log(col_mass)
     col_pot = jnp.zeros((cols,), jnp.float32)
     for iteration in range(ITERS):
         scores = affinity + (col_pot + log_train)[None, :]
@@ -124,20 +195,19 @@
         total = jnp.sum(weights, axis=0)
         local = highest + jnp.log(total)
         if iteration < ITERS - 1:
-            col_pot = -combine(exchange(local, "gen", n_gen))
+            col_pot = -combine(exchange(local, both, n_gen, groups))
     mean = jnp.sum(weights * affinity, axis=0) / total
-    small = 1 << 20
     (packed,) = call(
         pack_kernel,
         [shape(n_gen, 1, 2 * cols + LANES)],
         [local[None], mean[None], row_mass.reshape(-1, LANES)],
         limit=small,
     )
-    got = lax.all_to_all(packed, "gen", 0, 0)
+    got = lax.all_to_all(packed, both, 0, 0, axis_index_groups=groups)
     col_pot, gen_mass, packed = call(
         column_kernel,
-        [shape(1, cols), shape(1, LANES), shape(n_train, 1, 2 * LANES)],
-        [got, col_mass[None]],
+        [shape(1, cols), shape(1, LANES), shape(n_train, 1, 2 * LANES + cols)],
+        [got, tile_mass],
         limit=small,
     )
     got = lax.all_to_all(packed, "train", 0, 0)

time: 157 us -> 154 us (0.981)
  blocking collectives: 135 us -> 132 us
  Pallas kernels: 2.76 us -> 4.75 us
  local copies, waits for them, and re-layouts: 2.15 us -> 0.27 us
    all_to_all x6, blocking collectives: 91.9 us -> 85 us  [the longest x5 70.6 us: exchange(): return lax.all_to_all(copies, axis, 0, 0, axis_index_groups=groups)]
    all_gather x1, blocking collectives: 30.5 us -> 34.3 us  [shards(): lax.all_gather(train_embed, both, axis=0, tiled=True, axis_index_groups=g...]
    pallas_call x4 -> x5, Pallas kernels: 2.76 us -> 4.75 us  [call(): pl.pallas_call(kernel, out_shape=outs, in_specs=in_specs or [VMEM] * len(...]
    broadcast_in_dim x6 -> x5, local copies, waits for them, and re-layouts: 2.13 us -> 0.26 us  [exchange(): copies = jnp.broadcast_to(values[None], (count,) + values.shape)]
where the time goes in v5:
time: 154 us
  blocking collectives  132 us (86%)
  starting transfers between devices  10.5 us (7%)
  other arithmetic  5.38 us (3%)
  Pallas kernels  4.75 us (3%)
    all_to_all x5, blocking collectives, exchange(): return lax.all_to_all(copies, axis, 0, 0, axis_index_groups=groups)  70.6 us
    all_gather x1, blocking collectives, shards(): lax.all_gather(train_embed, both, axis=0, tiled=True, axis_index_groups=g...  34.3 us
    all_to_all x1, blocking collectives, shards(): got = lax.all_to_all(packed, both, 0, 0, axis_index_groups=groups)  14.4 us
    all_to_all x1, blocking collectives, shards(): got = lax.all_to_all(packed, 'train', 0, 0)  12.5 us
    all_to_all x1, starting transfers between devices, shards(): twice = 2.0 * lax.all_to_all(packed, 'train', 0, 0)  10.5 us
    pallas_call x5, Pallas kernels, call(): pl.pallas_call(kernel, out_shape=outs, in_specs=in_specs or [VMEM] * len(...  4.75 us
  transfers between devices with their start and end apart: 1, of which 0 were waited for; matrix products, arithmetic and copies ran while one was open for 0% of the time, Pallas kernels for 0%

profile of v5, /device:TPU:1, one launch (start us, length us, event | category | flops | bytes accessed | tf_op | source)
XLA Modules:
  0.0 153.5 jit_solution(2604292916467704939)
XLA Ops:
  0.6 1.9 %shard_map.67 = f32[32,40,256]{2,1,0:T(8,128)} custom-call(f32[32,256]{1,0:T(8,128)} %values.1, f32[1,512]{1,0:T(1,128)} %bitcast.48), custom_call_target="tpu_custom_call" | custom-call | tf_op jit(solution)/shard_map/pallas_call | solution.py:24
  2.6 10.5 %all-to-all-start = ((f32[32,40,256]{2,1,0:T(8,128)}), f32[32,40,256]{2,1,0:T(8,128)S(1)}, u32[]{:S(2)}, u32[]{:S(2)}) async-start(f32[32,40,256]{2,1,0:T(8,128)} %shard_map.67), calls=%async_computation | async-start | bytes 2621440 | tf_op jit(solution)/shard_map/all_to_all | solution.py:175
  13.1 34.3 %all_gather.3.train = f32[512,256]{1,0:T(8,128)S(1)} all-gather(f32[32,256]{1,0:T(8,128)S(1)} %copy-done.2), channel_id=1, replica_groups={{0,33,64,97,128,161,192,225,256,289,320,353,384,417,448,481},{1,32,65,9..., dimensions={0}, use_global_device_ids=true | all-gather | bytes 557056 | tf_op jit(solution)/shard_map/all_gather | solution.py:176
  47.4 0.1 multiply_reduce_fusion.1
  47.5 0.1 broadcast_multiply_fusion.twice
  47.6 2.0 %shard_map.68 = (f32[1024,512]{1,0:T(8,128)S(1)}, f32[1,512]{1,0:T(1,128)S(1)}, f32[1,512]{1,0:T(1,128)S(1)}) custom-call(f32[32,40,256]{2,1,0:T(8,128)S(1)} %broadcast_multiply_fusion.twice, f32[512,256]{1,0:T(8,128)S(1)} %all_gather.3.train, f32[1,512]{1,0:T(1,128)S(1)} %bitcast.50, f32[1,512]{1,0:T(1,128)S(1)} %bitcast.49), custom_call_target="tpu_custom_call" | custom-call | tf_op jit(solution)/shard_map/pallas_call | solution.py:24
  49.7 0.2 add_reduce_fusion.5
  49.9 0.6 exponential_reduce_fusion.4
  50.5 0.1 broadcast_in_dim.16
  50.6 14.3 %all_to_all.60 = f32[32,1,1024]{2,1,0:T(1,128)S(1)} all-to-all(f32[32,1,1024]{2,1,0:T(1,128)S(1)} %broadcast_in_dim.16), channel_id=1, replica_groups=mesh['gen'=16,'train'=32] {'train'}, dimensions={0} | all-to-all | bytes 262144 | tf_op jit(solution)/shard_map/all_to_all | solution.py:140
  64.9 0.1 reduce_max.100
  65.0 0.2 add_reduce_fusion.4
  65.2 0.4 exponential_reduce_fusion.3
  65.7 17.6 %all_to_all.61 = f32[16,1,512]{2,1,0:T(1,128)S(1)} all-to-all(f32[16,1,512]{2,1,0:T(1,128)S(1)} %broadcast_in_dim.17), channel_id=1, replica_groups={{0,33,64,97,128,161,192,225,256,289,320,353,384,417,448,481},{1,32,65,9..., dimensions={0} | all-to-all | bytes 65536 | tf_op jit(solution)/shard_map/all_to_all | solution.py:140
  83.4 0.2 add_reduce_fusion.3
  83.6 0.6 exponential_reduce_fusion.2
  84.2 0.1 broadcast_in_dim.18
  84.3 12.4 %all_to_all.62 = f32[32,1,1024]{2,1,0:T(1,128)S(1)} all-to-all(f32[32,1,1024]{2,1,0:T(1,128)S(1)} %broadcast_in_dim.18), channel_id=1, replica_groups=mesh['gen'=16,'train'=32] {'train'}, dimensions={0} | all-to-all | bytes 262144 | tf_op jit(solution)/shard_map/all_to_all | solution.py:140
  96.7 0.1 reduce_max.104
  96.9 0.2 add_reduce_fusion.2
  97.1 0.4 exponential_reduce_fusion.1
  97.6 13.8 %all_to_all.63 = f32[16,1,512]{2,1,0:T(1,128)S(1)} all-to-all(f32[16,1,512]{2,1,0:T(1,128)S(1)} %broadcast_in_dim.19), channel_id=1, replica_groups={{0,33,64,97,128,161,192,225,256,289,320,353,384,417,448,481},{1,32,65,9..., dimensions={0} | all-to-all | bytes 65536 | tf_op jit(solution)/shard_map/all_to_all | solution.py:140
  111.5 0.2 add_reduce_fusion.1
  111.8 0.6 exponential_reduce_fusion
  112.4 0.1 broadcast_in_dim.20
  112.4 12.5 %all_to_all.64 = f32[32,1,1024]{2,1,0:T(1,128)S(1)} all-to-all(f32[32,1,1024]{2,1,0:T(1,128)S(1)} %broadcast_in_dim.20), channel_id=1, replica_groups=mesh['gen'=16,'train'=32] {'train'}, dimensions={0} | all-to-all | bytes 262144 | tf_op jit(solution)/shard_map/all_to_all | solution.py:140
  124.9 0.1 reduce_max.108
  125.0 0.2 add_reduce_fusion
  125.3 0.6 multiply_reduce_fusion
  125.9 14.4 %all_to_all.65.got = f32[16,1,1152]{2,1,0:T(1,128)S(1)} all-to-all(f32[16,1,1152]{2,1,0:T(1,128)S(1)} %shard_map.69), channel_id=1, replica_groups={{0,33,64,97,128,161,192,225,256,289,320,353,384,417,448,481},{1,32,65,9..., dimensions={0} | all-to-all | bytes 147456 | tf_op jit(solution)/shard_map/all_to_all | solution.py:206
  140.4 12.5 %all_to_all.66.got = f32[32,1,768]{2,1,0:T(1,128)S(1)} all-to-all(f32[32,1,768]{2,1,0:T(1,128)S(1)} %get-tuple-element.15), channel_id=1, replica_groups=mesh['gen'=16,'train'=32] {'train'}, dimensions={0} | all-to-all | bytes 196608 | tf_op jit(solution)/shard_map/all_to_all | solution.py:213
  152.8 0.7 shard_map.71
  (31 shorter events, 0.5 us)
Async XLA Ops:
  0.6 12.4 %copy-start.2 = (f32[32,256]{1,0:T(8,128)S(1)}, f32[32,256]{1,0:T(8,128)}, u32[]{:S(2)}) copy-start(f32[32,256]{1,0:T(8,128)} %param.5) | copy-start | bytes 98308
  2.6 45.0 %all-to-all-start = ((f32[32,40,256]{2,1,0:T(8,128)}), f32[32,40,256]{2,1,0:T(8,128)S(1)}, u32[]{:S(2)}, u32[]{:S(2)}) async-start(f32[32,40,256]{2,1,0:T(8,128)} %shard_map.67), calls=%async_computation | async-start | bytes 2621440 | tf_op jit(solution)/shard_map/all_to_all | solution.py:175
  13.1 34.6 %copy-start.1 = (f32[512]{0:T(512)S(1)}, f32[512]{0:T(512)}, u32[]{:S(2)}) copy-start(f32[512]{0:T(512)} %param.7) | copy-start | bytes 6148
  49.7 15.3 %copy-start = (f32[1024]{0:T(1024)S(1)}, f32[1024]{0:T(1024)}, u32[]{:S(2)}) copy-start(f32[1024]{0:T(1024)} %param.6) | copy-start | bytes 12292

commit v6 on v5

--- a/solution.py
+++ b/solution.py
@@ -67,6 +67,11 @@
         move.wait()
 
 
+def halves(values):
+    high = values.astype(jnp.bfloat16)
+    return high, (values - high.astype(jnp.float32)).astype(jnp.bfloat16)
+
+
 def affinity_kernel(scale, twice, train, train_sq, mass, out, tile_mass, log_mass):
     members, _, width = twice.shape
     share = out.shape[0] // members
@@ -75,15 +80,15 @@
     masses = jnp.where(own(mass.shape), mass[...], other)
     tile_mass[...] = masses
     log_mass[...] = jnp.log(masses)
+    columns = halves(train[...])
     step = 8
     for start in range(0, members, step):
         part = twice[start : start + step, 0:share, :].reshape(step * share, width)
-        twice_inner = lax.dot_general(
-            part,
-            train[...],
-            (((1,), (1,)), ((), ())),
-            precision=lax.Precision.HIGHEST,
-            preferred_element_type=jnp.float32,
+        rows = halves(part)
+        twice_inner = sum(
+            lax.dot_general(left, right, (((1,), (1,)), ((), ())), preferred_element_type=jnp.float32)
+            for left in reversed(rows)
+            for right in reversed(columns)
         )
         part_sq = 0.25 * jnp.sum(part * part, axis=1, keepdims=True)
         out[start * share : (start + step) * share, :] = (twice_inner - part_sq - train_sq[...]) * scale

time: 154 us -> 153 us (level)
  no operation moved by 1% of the time
where the time goes in v6:
time: 153 us
  blocking collectives  132 us (86%)
  starting transfers between devices  10.5 us (7%)
  other arithmetic  5.38 us (4%)
  Pallas kernels  4.02 us (3%)
    all_to_all x5, blocking collectives, exchange(): return lax.all_to_all(copies, axis, 0, 0, axis_index_groups=groups)  70.6 us
    all_gather x1, blocking collectives, shards(): lax.all_gather(train_embed, both, axis=0, tiled=True, axis_index_groups=g...  34.3 us
    all_to_all x1, blocking collectives, shards(): got = lax.all_to_all(packed, both, 0, 0, axis_index_groups=groups)  14.4 us
    all_to_all x1, blocking collectives, shards(): got = lax.all_to_all(packed, 'train', 0, 0)  12.5 us
    all_to_all x1, starting transfers between devices, shards(): twice = 2.0 * lax.all_to_all(packed, 'train', 0, 0)  10.5 us
    pallas_call x5, Pallas kernels, call(): pl.pallas_call(kernel, out_shape=outs, in_specs=in_specs or [VMEM] * len(...  4.02 us
  transfers between devices with their start and end apart: 1, of which 0 were waited for; matrix products, arithmetic and copies ran while one was open for 0% of the time, Pallas kernels for 0%

profile of v6, /device:TPU:1, one launch (start us, length us, event | category | flops | bytes accessed | tf_op | source)
XLA Modules:
  0.0 152.8 jit_solution(1410489877811038838)
XLA Ops:
  0.6 1.9 %shard_map.67 = f32[32,40,256]{2,1,0:T(8,128)} custom-call(f32[32,256]{1,0:T(8,128)} %values.1, f32[1,512]{1,0:T(1,128)} %bitcast.48), custom_call_target="tpu_custom_call" | custom-call | tf_op jit(solution)/shard_map/pallas_call | solution.py:24
  2.6 10.5 %all-to-all-start = ((f32[32,40,256]{2,1,0:T(8,128)}), f32[32,40,256]{2,1,0:T(8,128)S(1)}, u32[]{:S(2)}, u32[]{:S(2)}) async-start(f32[32,40,256]{2,1,0:T(8,128)} %shard_map.67), calls=%async_computation | async-start | bytes 2621440 | tf_op jit(solution)/shard_map/all_to_all | solution.py:180
  13.1 34.3 %all_gather.3.train = f32[512,256]{1,0:T(8,128)S(1)} all-gather(f32[32,256]{1,0:T(8,128)S(1)} %copy-done.2), channel_id=1, replica_groups={{0,33,64,97,128,161,192,225,256,289,320,353,384,417,448,481},{1,32,65,9..., dimensions={0}, use_global_device_ids=true | all-gather | bytes 557056 | tf_op jit(solution)/shard_map/all_gather | solution.py:181
  47.4 0.1 multiply_reduce_fusion.1
  47.5 0.1 broadcast_multiply_fusion.twice
  47.6 1.3 shard_map.68
  49.0 0.2 add_reduce_fusion.5
  49.2 0.6 exponential_reduce_fusion.4
  49.8 0.1 broadcast_in_dim.16
  49.9 14.3 %all_to_all.60 = f32[32,1,1024]{2,1,0:T(1,128)S(1)} all-to-all(f32[32,1,1024]{2,1,0:T(1,128)S(1)} %broadcast_in_dim.16), channel_id=1, replica_groups=mesh['gen'=16,'train'=32] {'train'}, dimensions={0} | all-to-all | bytes 262144 | tf_op jit(solution)/shard_map/all_to_all | solution.py:145
  64.1 0.1 reduce_max.100
  64.3 0.2 add_reduce_fusion.4
  64.5 0.4 exponential_reduce_fusion.3
  65.0 17.6 %all_to_all.61 = f32[16,1,512]{2,1,0:T(1,128)S(1)} all-to-all(f32[16,1,512]{2,1,0:T(1,128)S(1)} %broadcast_in_dim.17), channel_id=1, replica_groups={{0,33,64,97,128,161,192,225,256,289,320,353,384,417,448,481},{1,32,65,9..., dimensions={0} | all-to-all | bytes 65536 | tf_op jit(solution)/shard_map/all_to_all | solution.py:145
  82.7 0.2 add_reduce_fusion.3
  82.9 0.6 exponential_reduce_fusion.2
  83.5 0.1 broadcast_in_dim.18
  83.6 12.4 %all_to_all.62 = f32[32,1,1024]{2,1,0:T(1,128)S(1)} all-to-all(f32[32,1,1024]{2,1,0:T(1,128)S(1)} %broadcast_in_dim.18), channel_id=1, replica_groups=mesh['gen'=16,'train'=32] {'train'}, dimensions={0} | all-to-all | bytes 262144 | tf_op jit(solution)/shard_map/all_to_all | solution.py:145
  96.0 0.1 reduce_max.104
  96.2 0.2 add_reduce_fusion.2
  96.4 0.4 exponential_reduce_fusion.1
  96.9 13.8 %all_to_all.63 = f32[16,1,512]{2,1,0:T(1,128)S(1)} all-to-all(f32[16,1,512]{2,1,0:T(1,128)S(1)} %broadcast_in_dim.19), channel_id=1, replica_groups={{0,33,64,97,128,161,192,225,256,289,320,353,384,417,448,481},{1,32,65,9..., dimensions={0} | all-to-all | bytes 65536 | tf_op jit(solution)/shard_map/all_to_all | solution.py:145
  110.8 0.2 add_reduce_fusion.1
  111.0 0.6 exponential_reduce_fusion
  111.6 0.1 broadcast_in_dim.20
  111.7 12.5 %all_to_all.64 = f32[32,1,1024]{2,1,0:T(1,128)S(1)} all-to-all(f32[32,1,1024]{2,1,0:T(1,128)S(1)} %broadcast_in_dim.20), channel_id=1, replica_groups=mesh['gen'=16,'train'=32] {'train'}, dimensions={0} | all-to-all | bytes 262144 | tf_op jit(solution)/shard_map/all_to_all | solution.py:145
  124.2 0.1 reduce_max.108
  124.3 0.2 add_reduce_fusion
  124.5 0.6 multiply_reduce_fusion
  125.1 14.4 %all_to_all.65.got = f32[16,1,1152]{2,1,0:T(1,128)S(1)} all-to-all(f32[16,1,1152]{2,1,0:T(1,128)S(1)} %shard_map.69), channel_id=1, replica_groups={{0,33,64,97,128,161,192,225,256,289,320,353,384,417,448,481},{1,32,65,9..., dimensions={0} | all-to-all | bytes 147456 | tf_op jit(solution)/shard_map/all_to_all | solution.py:211
  139.6 12.5 %all_to_all.66.got = f32[32,1,768]{2,1,0:T(1,128)S(1)} all-to-all(f32[32,1,768]{2,1,0:T(1,128)S(1)} %get-tuple-element.15), channel_id=1, replica_groups=mesh['gen'=16,'train'=32] {'train'}, dimensions={0} | all-to-all | bytes 196608 | tf_op jit(solution)/shard_map/all_to_all | solution.py:218
  152.1 0.7 shard_map.71
  (31 shorter events, 0.5 us)
Async XLA Ops:
  0.6 12.4 %copy-start.2 = (f32[32,256]{1,0:T(8,128)S(1)}, f32[32,256]{1,0:T(8,128)}, u32[]{:S(2)}) copy-start(f32[32,256]{1,0:T(8,128)} %param.5) | copy-start | bytes 98308
  2.6 45.0 %all-to-all-start = ((f32[32,40,256]{2,1,0:T(8,128)}), f32[32,40,256]{2,1,0:T(8,128)S(1)}, u32[]{:S(2)}, u32[]{:S(2)}) async-start(f32[32,40,256]{2,1,0:T(8,128)} %shard_map.67), calls=%async_computation | async-start | bytes 2621440 | tf_op jit(solution)/shard_map/all_to_all | solution.py:180
  13.1 34.6 %copy-start.1 = (f32[512]{0:T(512)S(1)}, f32[512]{0:T(512)}, u32[]{:S(2)}) copy-start(f32[512]{0:T(512)} %param.7) | copy-start | bytes 6148
  49.0 15.3 %copy-start = (f32[1024]{0:T(1024)S(1)}, f32[1024]{0:T(1024)}, u32[]{:S(2)}) copy-start(f32[1024]{0:T(1024)} %param.6) | copy-start | bytes 12292

commit v7 on v6

--- a/solution.py
+++ b/solution.py
@@ -72,15 +72,85 @@
     return high, (values - high.astype(jnp.float32)).astype(jnp.bfloat16)
 
 
-def affinity_kernel(scale, twice, train, train_sq, mass, out, tile_mass, log_mass):
+def combined(got, cols):
+    logs = [got[k, :, 0:cols] for k in range(got.shape[0])]
+    highest = functools.reduce(jnp.maximum, logs)
+    return highest + jnp.log(sum(jnp.exp(log - highest) for log in logs))
+
+
+def row_logs(block, weights):
+    pieces = []
+    for at in range(0, block.shape[0], LANES):
+        scores = block[at : at + LANES, :] + weights
+        highest = jnp.max(scores, axis=1, keepdims=True)
+        total = jnp.sum(jnp.exp(scores - highest), axis=1, keepdims=True)
+        pieces.append(jnp.broadcast_to(highest + jnp.log(total), (LANES, LANES)).T[0:1, :])
+    return pieces
+
+
+def send(pieces, out):
+    whole = jnp.concatenate(pieces, axis=1)
+    for k in range(out.shape[0]):
+        out[k] = whole
+
+
+def train_kernel(got, log_train, affinity, out):
+    send(row_logs(affinity, log_train[...] - combined(got, log_train.shape[1])), out)
+
+
+def gen_kernel(last, got, mass, affinity, *outs):
+    rows, cols = affinity.shape
+    out, offsets = outs[-2:]
+    potential = -combined(got, rows)
+    if last:
+        outs[0][...] = potential
+    weights = potential + jnp.log(mass[...])
+    lanes = cols // LANES
+    sub = 8
+
+    def fold(reduce, block):
+        return reduce(block.reshape(LANES // sub, sub, cols), axis=0)
+
+    def scores(at):
+        return affinity[at : at + LANES, :] + jnp.concatenate([offsets[at : at + LANES, :]] * lanes, axis=1)
+
+    highest = None
+    for at in range(0, rows, LANES):
+        offsets[at : at + LANES, :] = jnp.broadcast_to(weights[:, at : at + LANES], (LANES, LANES)).T
+        part = fold(jnp.max, scores(at))
+        highest = part if highest is None else jnp.maximum(highest, part)
+    highest = jnp.max(highest, axis=0, keepdims=True)
+    total = mean = jnp.zeros((sub, cols), jnp.float32)
+    for at in range(0, rows, LANES):
+        share = jnp.exp(scores(at) - highest)
+        total += fold(jnp.sum, share)
+        if last:
+            mean += fold(jnp.sum, share * affinity[at : at + LANES, :])
+    total = jnp.sum(total, axis=0, keepdims=True)
+    logs = highest + jnp.log(total)
+    if last:
+        mean = jnp.sum(mean, axis=0, keepdims=True) / total
+        masses = sum(mass[:, at : at + LANES] for at in range(0, rows, LANES))
+        send([logs, mean, masses], out)
+    else:
+        send([logs], out)
+
+
+def affinity_kernel(scale, twice, train, train_sq, out, tile_mass, log_mass, logs):
     members, _, width = twice.shape
     share = out.shape[0] // members
-    other = twice[partner(), share : share + mass.shape[1] // width, :]
-    other = 0.5 * jnp.concatenate([other[k : k + 1] for k in range(other.shape[0])], axis=1)
-    masses = jnp.where(own(mass.shape), mass[...], other)
+    cols = out.shape[1]
+
+    def mass_of(member):
+        held = twice[member, share : share + cols // width, :]
+        return 0.5 * jnp.concatenate([held[k : k + 1] for k in range(cols // width)], axis=1)
+
+    masses = jnp.where(own((1, cols)), mass_of(lax.axis_index("train")), mass_of(partner()))
     tile_mass[...] = masses
-    log_mass[...] = jnp.log(masses)
+    weights = jnp.log(masses)
+    log_mass[...] = weights
     columns = halves(train[...])
+    pieces = []
     step = 8
     for start in range(0, members, step):
         part = twice[start : start + step, 0:share, :].reshape(step * share, width)
@@ -91,16 +161,10 @@
             for right in reversed(columns)
         )
         part_sq = 0.25 * jnp.sum(part * part, axis=1, keepdims=True)
-        out[start * share : (start + step) * share, :] = (twice_inner - part_sq - train_sq[...]) * scale
-
-
-def pack_kernel(local, mean, mass, out):
-    cols = local.shape[1]
-    total = jnp.sum(mass[...], axis=0, keepdims=True)
-    for k in range(out.shape[0]):
-        out[k, :, 0:cols] = local[...]
-        out[k, :, cols : 2 * cols] = mean[...]
-        out[k, :, 2 * cols :] = total
+        block = (twice_inner - part_sq - train_sq[...]) * scale
+        out[start * share : (start + step) * share, :] = block
+        pieces += row_logs(block, weights)
+    send(pieces, logs)
 
 
 def column_kernel(got, mass, col_pot, gen_mass, out):
@@ -138,16 +202,6 @@
     row_out[...] = EPSILON * (row_pot[...] + (ITERS * log_train - (ITERS - 1) * log_gen))
     col_out[...] = EPSILON * (columns + ITERS * (log_gen - log_train))
     cost_out[...] = -EPSILON * cost / train_total
-
-
-def exchange(values, axis, count, groups=None):
-    copies = jnp.broadcast_to(values[None], (count,) + values.shape)
-    return lax.all_to_all(copies, axis, 0, 0, axis_index_groups=groups)
-
-
-def combine(logs):
-    highest = jnp.max(logs, axis=0)
-    return highest + jnp.log(jnp.sum(jnp.exp(logs - highest[None]), axis=0))
 
 
 def shards(n_gen, n_train, gen_embed, train_embed, row_mass, col_mass):
@@ -180,35 +234,24 @@
     twice = 2.0 * lax.all_to_all(packed, "train", 0, 0)
     train_block = lax.all_gather(train_embed, both, axis=0, tiled=True, axis_index_groups=groups)
     train_sq = jnp.sum(train_block * train_block, axis=1)
-    affinity, tile_mass, log_train = call(
+    affinity, tile_mass, log_train, packed = call(
         functools.partial(affinity_kernel, 1.0 / (width * EPSILON)),
-        [shape(rows, cols), shape(1, cols), shape(1, cols)],
-        [twice, train_block, train_sq[None], col_mass[None]],
-    )
-    log_train = log_train[0]
-
-    log_gen = jnp.log(row_mass)
-    col_pot = jnp.zeros((cols,), jnp.float32)
+        [shape(rows, cols), shape(1, cols), shape(1, cols), shape(n_train, 1, rows)],
+        [twice, train_block, train_sq[None]],
+    )
+
     for iteration in range(ITERS):
-        scores = affinity + (col_pot + log_train)[None, :]
-        highest = jnp.max(scores, axis=1)
-        local = highest + jnp.log(jnp.sum(jnp.exp(scores - highest[:, None]), axis=1))
-        row_pot = -combine(exchange(local, "train", n_train))
-        scores = affinity + (row_pot + log_gen)[:, None]
-        highest = jnp.max(scores, axis=0)
-        weights = jnp.exp(scores - highest[None, :])
-        total = jnp.sum(weights, axis=0)
-        local = highest + jnp.log(total)
-        if iteration < ITERS - 1:
-            col_pot = -combine(exchange(local, both, n_gen, groups))
-    mean = jnp.sum(weights * affinity, axis=0) / total
-    (packed,) = call(
-        pack_kernel,
-        [shape(n_gen, 1, 2 * cols + LANES)],
-        [local[None], mean[None], row_mass.reshape(-1, LANES)],
-        limit=small,
-    )
-    got = lax.all_to_all(packed, both, 0, 0, axis_index_groups=groups)
+        last = iteration == ITERS - 1
+        got = lax.all_to_all(packed, "train", 0, 0)
+        *row_pot, packed = call(
+            functools.partial(gen_kernel, last),
+            [shape(1, rows), shape(n_gen, 1, 2 * cols + LANES)] if last else [shape(n_gen, 1, cols)],
+            [got, row_mass[None], affinity],
+            scratch=[pltpu.VMEM((rows, LANES), jnp.float32)],
+        )
+        got = lax.all_to_all(packed, both, 0, 0, axis_index_groups=groups)
+        if not last:
+            (packed,) = call(train_kernel, [shape(n_train, 1, rows)], [got, log_train, affinity])
     col_pot, gen_mass, packed = call(
         column_kernel,
         [shape(1, cols), shape(1, LANES), shape(n_train, 1, 2 * LANES + cols)],
@@ -218,8 +261,8 @@
     got = lax.all_to_all(packed, "train", 0, 0)
     row_out, col_out, cost = call(
         outputs_kernel,
-        [shape(rows // LANES, LANES), shape(1, cols), shape(1, 1)],
-        [got, row_pot.reshape(-1, LANES), col_pot, gen_mass],
+        [shape(1, rows), shape(1, cols), shape(1, 1)],
+        [got, *row_pot, col_pot, gen_mass],
         limit=small,
     )
     return (row_out.reshape(rows), col_out.reshape(cols), cost.reshape(()))

time: 153 us -> 152 us (level)
  other arithmetic: 5.38 us -> 0.23 us
  Pallas kernels: 4.02 us -> 8.2 us
    all_to_all x5 -> x0, blocking collectives: 70.6 us -> none  [exchange(): return lax.all_to_all(copies, axis, 0, 0, axis_index_groups=groups)]
    all_to_all x1 -> x4, blocking collectives: 12.5 us -> 51.5 us  [shards(): got = lax.all_to_all(packed, 'train', 0, 0)]
    all_to_all x1 -> x3, blocking collectives: 14.4 us -> 46.2 us  [shards(): got = lax.all_to_all(packed, both, 0, 0, axis_index_groups=groups)]
    pallas_call x5 -> x9, Pallas kernels: 4.02 us -> 8.2 us  [call(): pl.pallas_call(kernel, out_shape=outs, in_specs=in_specs or [VMEM] * len(...]
    reduce_sum x11 -> x0, other arithmetic: 3.37 us -> none  [the longest x3 1.74 us: shards(): jnp.sum(jnp.exp(scores - highest[:, None]), axis=1)]
    reduce_max x11 -> x0, other arithmetic: 1.68 us -> none  [the longest x3 0.66 us: shards(): highest = jnp.max(scores, axis=0)]
where the time goes in v7:
time: 152 us
  blocking collectives  132 us (87%)
  starting transfers between devices  10.5 us (7%)
  Pallas kernels  8.2 us (5%)
    all_to_all x4, blocking collectives, shards(): got = lax.all_to_all(packed, 'train', 0, 0)  51.5 us
    all_to_all x3, blocking collectives, shards(): got = lax.all_to_all(packed, both, 0, 0, axis_index_groups=groups)  46.2 us
    all_gather x1, blocking collectives, shards(): lax.all_gather(train_embed, both, axis=0, tiled=True, axis_index_groups=g...  34.3 us
    all_to_all x1, starting transfers between devices, shards(): twice = 2.0 * lax.all_to_all(packed, 'train', 0, 0)  10.5 us
    pallas_call x9, Pallas kernels, call(): pl.pallas_call(kernel, out_shape=outs, in_specs=in_specs or [VMEM] * len(...  8.2 us
  transfers between devices with their start and end apart: 1, of which 0 were waited for; matrix products, arithmetic and copies ran while one was open for 0% of the time, Pallas kernels for 0%

profile of v7, /device:TPU:1, one launch (start us, length us, event | category | flops | bytes accessed | tf_op | source)
XLA Modules:
  0.0 151.7 jit_solution(10777706873887296309)
XLA Ops:
  0.6 1.9 %shard_map.67 = f32[32,40,256]{2,1,0:T(8,128)} custom-call(f32[32,256]{1,0:T(8,128)} %values.1, f32[1,512]{1,0:T(1,128)} %bitcast.10), custom_call_target="tpu_custom_call" | custom-call | tf_op jit(solution)/shard_map/pallas_call | solution.py:24
  2.6 0.0 copy-start.1
  2.6 10.5 %all-to-all-start = ((f32[32,40,256]{2,1,0:T(8,128)}), f32[32,40,256]{2,1,0:T(8,128)S(1)}, u32[]{:S(2)}, u32[]{:S(2)}) async-start(f32[32,40,256]{2,1,0:T(8,128)} %shard_map.67), calls=%async_computation | async-start | bytes 2621440 | tf_op jit(solution)/shard_map/all_to_all | solution.py:234
  13.1 0.0 copy-done.1
  13.1 34.3 %all_gather.3.train = f32[512,256]{1,0:T(8,128)S(1)} all-gather(f32[32,256]{1,0:T(8,128)S(1)} %copy-done.1), channel_id=1, replica_groups={{0,33,64,97,128,161,192,225,256,289,320,353,384,417,448,481},{1,32,65,9..., dimensions={0}, use_global_device_ids=true | all-gather | bytes 557056 | tf_op jit(solution)/shard_map/all_gather | solution.py:235
  47.4 0.1 multiply_reduce_fusion
  47.5 0.0 all-to-all-done
  47.5 0.1 broadcast_multiply_fusion.twice
  47.6 0.0 copy-start
  47.6 1.6 %shard_map.68 = (f32[1024,512]{1,0:T(8,128)S(1)}, f32[1,512]{1,0:T(1,128)S(1)}, f32[1,512]{1,0:T(1,128)S(1)}, f32[32,1,1024]{2,1,0:T(1,128)S(1)}) custom-call(f32[32,40,256]{2,1,0:T(8,128)S(1)} %broadcast_multiply_fusion.twice, f32[512,256]{1,0:T(8,128)S(1)} %all_gather.3.train, f32[1,512]{1,0:T(1,128)S(1)} %bitcast.9), custom_call_target="tpu_custom_call" | custom-call | tf_op jit(solution)/shard_map/pallas_call | solution.py:24
  49.3 13.9 %all_to_all.40.got = f32[32,1,1024]{2,1,0:T(1,128)S(1)} all-to-all(f32[32,1,1024]{2,1,0:T(1,128)S(1)} %get-tuple-element.15), channel_id=1, replica_groups=mesh['gen'=16,'train'=32] {'train'}, dimensions={0} | all-to-all | bytes 262144 | tf_op jit(solution)/shard_map/all_to_all | solution.py:245
  63.2 0.0 copy-done
  63.2 0.6 shard_map.69
  63.8 18.0 %all_to_all.41.got = f32[16,1,512]{2,1,0:T(1,128)S(1)} all-to-all(f32[16,1,512]{2,1,0:T(1,128)S(1)} %shard_map.69), channel_id=1, replica_groups={{0,33,64,97,128,161,192,225,256,289,320,353,384,417,448,481},{1,32,65,9..., dimensions={0} | all-to-all | bytes 65536 | tf_op jit(solution)/shard_map/all_to_all | solution.py:252
  81.8 0.9 shard_map.70
  82.7 12.6 %all_to_all.42.got = f32[32,1,1024]{2,1,0:T(1,128)S(1)} all-to-all(f32[32,1,1024]{2,1,0:T(1,128)S(1)} %shard_map.70), channel_id=1, replica_groups=mesh['gen'=16,'train'=32] {'train'}, dimensions={0} | all-to-all | bytes 262144 | tf_op jit(solution)/shard_map/all_to_all | solution.py:245
  95.3 0.6 shard_map.71
  95.9 13.8 %all_to_all.43.got = f32[16,1,512]{2,1,0:T(1,128)S(1)} all-to-all(f32[16,1,512]{2,1,0:T(1,128)S(1)} %shard_map.71), channel_id=1, replica_groups={{0,33,64,97,128,161,192,225,256,289,320,353,384,417,448,481},{1,32,65,9..., dimensions={0} | all-to-all | bytes 65536 | tf_op jit(solution)/shard_map/all_to_all | solution.py:252
  109.8 0.9 shard_map.72
  110.7 12.5 %all_to_all.44.got = f32[32,1,1024]{2,1,0:T(1,128)S(1)} all-to-all(f32[32,1,1024]{2,1,0:T(1,128)S(1)} %shard_map.72), channel_id=1, replica_groups=mesh['gen'=16,'train'=32] {'train'}, dimensions={0} | all-to-all | bytes 262144 | tf_op jit(solution)/shard_map/all_to_all | solution.py:245
  123.2 0.8 shard_map.73
  124.0 14.4 %all_to_all.45.got = f32[16,1,1152]{2,1,0:T(1,128)S(1)} all-to-all(f32[16,1,1152]{2,1,0:T(1,128)S(1)} %get-tuple-element.18), channel_id=1, replica_groups={{0,33,64,97,128,161,192,225,256,289,320,353,384,417,448,481},{1,32,65,9..., dimensions={0} | all-to-all | bytes 147456 | tf_op jit(solution)/shard_map/all_to_all | solution.py:252
  138.4 0.1 shard_map.74
  138.5 12.5 %all_to_all.46.got = f32[32,1,768]{2,1,0:T(1,128)S(1)} all-to-all(f32[32,1,768]{2,1,0:T(1,128)S(1)} %get-tuple-element.20), channel_id=1, replica_groups=mesh['gen'=16,'train'=32] {'train'}, dimensions={0} | all-to-all | bytes 196608 | tf_op jit(solution)/shard_map/all_to_all | solution.py:261
  151.0 0.7 shard_map.75
Async XLA Ops:
  2.6 10.5 %copy-start.1 = (f32[32,256]{1,0:T(8,128)S(1)}, f32[32,256]{1,0:T(8,128)}, u32[]{:S(2)}) copy-start(f32[32,256]{1,0:T(8,128)} %param.5) | copy-start | bytes 98308
  2.6 45.0 %all-to-all-start = ((f32[32,40,256]{2,1,0:T(8,128)}), f32[32,40,256]{2,1,0:T(8,128)S(1)}, u32[]{:S(2)}, u32[]{:S(2)}) async-start(f32[32,40,256]{2,1,0:T(8,128)} %shard_map.67), calls=%async_computation | async-start | bytes 2621440 | tf_op jit(solution)/shard_map/all_to_all | solution.py:234
  47.6 15.5 %copy-start = (f32[1024]{0:T(1024)S(1)}, f32[1024]{0:T(1024)}, u32[]{:S(2)}) copy-start(f32[1024]{0:T(1024)} %param.6) | copy-start | bytes 12292

commit v8 on v7

--- a/solution.py
+++ b/solution.py
@@ -79,13 +79,15 @@
 
 
 def row_logs(block, weights):
-    pieces = []
-    for at in range(0, block.shape[0], LANES):
-        scores = block[at : at + LANES, :] + weights
-        highest = jnp.max(scores, axis=1, keepdims=True)
-        total = jnp.sum(jnp.exp(scores - highest), axis=1, keepdims=True)
-        pieces.append(jnp.broadcast_to(highest + jnp.log(total), (LANES, LANES)).T[0:1, :])
-    return pieces
+    starts = range(0, block.shape[0], LANES)
+
+    def scores(at):
+        return block[at : at + LANES, :] + weights
+
+    highest = [jnp.max(scores(at), axis=1, keepdims=True) for at in starts]
+    totals = [jnp.sum(jnp.exp(scores(at) - high), axis=1, keepdims=True) for at, high in zip(starts, highest)]
+    logs = [high + jnp.log(total) for high, total in zip(highest, totals)]
+    return [jnp.broadcast_to(log, (LANES, LANES)).T[0:1, :] for log in logs]
 
 
 def send(pieces, out):

time: 152 us -> 152 us (level)
  no operation moved by 1% of the time
where the time goes in v8:
time: 152 us; the launch traced here: 151 us
  blocking collectives  132 us (87%)
  starting transfers between devices  10.5 us (7%)
  Pallas kernels  7.78 us (5%)
    all_to_all x4, blocking collectives, shards(): got = lax.all_to_all(packed, 'train', 0, 0)  51.5 us
    all_to_all x3, blocking collectives, shards(): got = lax.all_to_all(packed, both, 0, 0, axis_index_groups=groups)  46.2 us
    all_gather x1, blocking collectives, shards(): lax.all_gather(train_embed, both, axis=0, tiled=True, axis_index_groups=g...  34.3 us
    all_to_all x1, starting transfers between devices, shards(): twice = 2.0 * lax.all_to_all(packed, 'train', 0, 0)  10.5 us
    pallas_call x9, Pallas kernels, call(): pl.pallas_call(kernel, out_shape=outs, in_specs=in_specs or [VMEM] * len(...  7.78 us
  transfers between devices with their start and end apart: 1, of which 0 were waited for; matrix products, arithmetic and copies ran while one was open for 0% of the time, Pallas kernels for 0%

profile of v8, /device:TPU:1, one launch (start us, length us, event | category | flops | bytes accessed | tf_op | source)
XLA Modules:
  0.0 151.3 jit_solution(18087559739501318736)
XLA Ops:
  0.6 1.9 %shard_map.67 = f32[32,40,256]{2,1,0:T(8,128)} custom-call(f32[32,256]{1,0:T(8,128)} %values.1, f32[1,512]{1,0:T(1,128)} %bitcast.10), custom_call_target="tpu_custom_call" | custom-call | tf_op jit(solution)/shard_map/pallas_call | solution.py:24
  2.6 0.0 copy-start.1
  2.6 10.5 %all-to-all-start = ((f32[32,40,256]{2,1,0:T(8,128)}), f32[32,40,256]{2,1,0:T(8,128)S(1)}, u32[]{:S(2)}, u32[]{:S(2)}) async-start(f32[32,40,256]{2,1,0:T(8,128)} %shard_map.67), calls=%async_computation | async-start | bytes 2621440 | tf_op jit(solution)/shard_map/all_to_all | solution.py:236
  13.1 0.0 copy-done.1
  13.1 34.3 %all_gather.3.train = f32[512,256]{1,0:T(8,128)S(1)} all-gather(f32[32,256]{1,0:T(8,128)S(1)} %copy-done.1), channel_id=1, replica_groups={{0,33,64,97,128,161,192,225,256,289,320,353,384,417,448,481},{1,32,65,9..., dimensions={0}, use_global_device_ids=true | all-gather | bytes 557056 | tf_op jit(solution)/shard_map/all_gather | solution.py:237
  47.4 0.1 multiply_reduce_fusion
  47.5 0.0 all-to-all-done
  47.5 0.1 broadcast_multiply_fusion.twice
  47.6 0.0 copy-start
  47.6 1.7 %shard_map.68 = (f32[1024,512]{1,0:T(8,128)S(1)}, f32[1,512]{1,0:T(1,128)S(1)}, f32[1,512]{1,0:T(1,128)S(1)}, f32[32,1,1024]{2,1,0:T(1,128)S(1)}) custom-call(f32[32,40,256]{2,1,0:T(8,128)S(1)} %broadcast_multiply_fusion.twice, f32[512,256]{1,0:T(8,128)S(1)} %all_gather.3.train, f32[1,512]{1,0:T(1,128)S(1)} %bitcast.9), custom_call_target="tpu_custom_call" | custom-call | tf_op jit(solution)/shard_map/pallas_call | solution.py:24
  49.3 13.9 %all_to_all.40.got = f32[32,1,1024]{2,1,0:T(1,128)S(1)} all-to-all(f32[32,1,1024]{2,1,0:T(1,128)S(1)} %get-tuple-element.15), channel_id=1, replica_groups=mesh['gen'=16,'train'=32] {'train'}, dimensions={0} | all-to-all | bytes 262144 | tf_op jit(solution)/shard_map/all_to_all | solution.py:247
  63.2 0.0 copy-done
  63.2 0.6 shard_map.69
  63.8 18.0 %all_to_all.41.got = f32[16,1,512]{2,1,0:T(1,128)S(1)} all-to-all(f32[16,1,512]{2,1,0:T(1,128)S(1)} %shard_map.69), channel_id=1, replica_groups={{0,33,64,97,128,161,192,225,256,289,320,353,384,417,448,481},{1,32,65,9..., dimensions={0} | all-to-all | bytes 65536 | tf_op jit(solution)/shard_map/all_to_all | solution.py:254
  81.8 0.7 shard_map.70
  82.5 12.6 %all_to_all.42.got = f32[32,1,1024]{2,1,0:T(1,128)S(1)} all-to-all(f32[32,1,1024]{2,1,0:T(1,128)S(1)} %shard_map.70), channel_id=1, replica_groups=mesh['gen'=16,'train'=32] {'train'}, dimensions={0} | all-to-all | bytes 262144 | tf_op jit(solution)/shard_map/all_to_all | solution.py:247
  95.1 0.6 shard_map.71
  95.7 13.8 %all_to_all.43.got = f32[16,1,512]{2,1,0:T(1,128)S(1)} all-to-all(f32[16,1,512]{2,1,0:T(1,128)S(1)} %shard_map.71), channel_id=1, replica_groups={{0,33,64,97,128,161,192,225,256,289,320,353,384,417,448,481},{1,32,65,9..., dimensions={0} | all-to-all | bytes 65536 | tf_op jit(solution)/shard_map/all_to_all | solution.py:254
  109.6 0.7 shard_map.72
  110.3 12.5 %all_to_all.44.got = f32[32,1,1024]{2,1,0:T(1,128)S(1)} all-to-all(f32[32,1,1024]{2,1,0:T(1,128)S(1)} %shard_map.72), channel_id=1, replica_groups=mesh['gen'=16,'train'=32] {'train'}, dimensions={0} | all-to-all | bytes 262144 | tf_op jit(solution)/shard_map/all_to_all | solution.py:247
  122.8 0.8 shard_map.73
  123.6 14.4 %all_to_all.45.got = f32[16,1,1152]{2,1,0:T(1,128)S(1)} all-to-all(f32[16,1,1152]{2,1,0:T(1,128)S(1)} %get-tuple-element.18), channel_id=1, replica_groups={{0,33,64,97,128,161,192,225,256,289,320,353,384,417,448,481},{1,32,65,9..., dimensions={0} | all-to-all | bytes 147456 | tf_op jit(solution)/shard_map/all_to_all | solution.py:254
  138.0 0.1 shard_map.74
  138.1 12.5 %all_to_all.46.got = f32[32,1,768]{2,1,0:T(1,128)S(1)} all-to-all(f32[32,1,768]{2,1,0:T(1,128)S(1)} %get-tuple-element.20), channel_id=1, replica_groups=mesh['gen'=16,'train'=32] {'train'}, dimensions={0} | all-to-all | bytes 196608 | tf_op jit(solution)/shard_map/all_to_all | solution.py:263
  150.6 0.7 shard_map.75
Async XLA Ops:
  2.6 10.5 %copy-start.1 = (f32[32,256]{1,0:T(8,128)S(1)}, f32[32,256]{1,0:T(8,128)}, u32[]{:S(2)}) copy-start(f32[32,256]{1,0:T(8,128)} %param.5) | copy-start | bytes 98308
  2.6 45.0 %all-to-all-start = ((f32[32,40,256]{2,1,0:T(8,128)}), f32[32,40,256]{2,1,0:T(8,128)S(1)}, u32[]{:S(2)}, u32[]{:S(2)}) async-start(f32[32,40,256]{2,1,0:T(8,128)} %shard_map.67), calls=%async_computation | async-start | bytes 2621440 | tf_op jit(solution)/shard_map/all_to_all | solution.py:236
  47.6 15.6 %copy-start = (f32[1024]{0:T(1024)S(1)}, f32[1024]{0:T(1024)}, u32[]{:S(2)}) copy-start(f32[1024]{0:T(1024)} %param.6) | copy-start | bytes 12292

commit v9 on v8

--- a/solution.py
+++ b/solution.py
@@ -138,7 +138,7 @@
         send([logs], out)
 
 
-def affinity_kernel(scale, twice, train, train_sq, out, tile_mass, log_mass, logs):
+def affinity_kernel(scale, twice, train, out, tile_mass, log_mass, logs):
     members, _, width = twice.shape
     share = out.shape[0] // members
     cols = out.shape[1]
@@ -152,6 +152,9 @@
     weights = jnp.log(masses)
     log_mass[...] = weights
     columns = halves(train[...])
+    squares = [train[at : at + LANES, :] * train[at : at + LANES, :] for at in range(0, cols, LANES)]
+    squares = [jnp.sum(part, axis=1, keepdims=True) for part in squares]
+    train_sq = jnp.concatenate([jnp.broadcast_to(part, (LANES, LANES)).T[0:1, :] for part in squares], axis=1)
     pieces = []
     step = 8
     for start in range(0, members, step):
@@ -163,7 +166,7 @@
             for right in reversed(columns)
         )
         part_sq = 0.25 * jnp.sum(part * part, axis=1, keepdims=True)
-        block = (twice_inner - part_sq - train_sq[...]) * scale
+        block = (twice_inner - part_sq - train_sq) * scale
         out[start * share : (start + step) * share, :] = block
         pieces += row_logs(block, weights)
     send(pieces, logs)
@@ -217,7 +220,7 @@
     ]
     small = 1 << 20
     height = gen_embed.shape[0] + 8
-    many = 4
+    many = 8
     (packed,) = call(
         copies_kernel,
         [shape(n_train, height, width)],
@@ -235,11 +238,10 @@
     )
     twice = 2.0 * lax.all_to_all(packed, "train", 0, 0)
     train_block = lax.all_gather(train_embed, both, axis=0, tiled=True, axis_index_groups=groups)
-    train_sq = jnp.sum(train_block * train_block, axis=1)
     affinity, tile_mass, log_train, packed = call(
         functools.partial(affinity_kernel, 1.0 / (width * EPSILON)),
         [shape(rows, cols), shape(1, cols), shape(1, cols), shape(n_train, 1, rows)],
-        [twice, train_block, train_sq[None]],
+        [twice, train_block],
     )
 
     for iteration in range(ITERS):

time: 152 us -> 152 us (level)
  no operation moved by 1% of the time
where the time goes in v9:
time: 152 us; the launch traced here: 151 us
  blocking collectives  132 us (87%)
  starting transfers between devices  10.5 us (7%)
  Pallas kernels  7.74 us (5%)
    all_to_all x4, blocking collectives, shards(): got = lax.all_to_all(packed, 'train', 0, 0)  51.5 us
    all_to_all x3, blocking collectives, shards(): got = lax.all_to_all(packed, both, 0, 0, axis_index_groups=groups)  46.2 us
    all_gather x1, blocking collectives, shards(): lax.all_gather(train_embed, both, axis=0, tiled=True, axis_index_groups=g...  34.3 us
    all_to_all x1, starting transfers between devices, shards(): twice = 2.0 * lax.all_to_all(packed, 'train', 0, 0)  10.5 us
    pallas_call x9, Pallas kernels, call(): pl.pallas_call(kernel, out_shape=outs, in_specs=in_specs or [VMEM] * len(...  7.74 us
  transfers between devices with their start and end apart: 1, of which 0 were waited for; matrix products, arithmetic and copies ran while one was open for 0% of the time, Pallas kernels for 0%

profile of v9, /device:TPU:1, one launch (start us, length us, event | category | flops | bytes accessed | tf_op | source)
XLA Modules:
  0.0 151.1 jit_solution(11751105784594012721)
XLA Ops:
  0.6 1.9 %shard_map.67 = f32[32,40,256]{2,1,0:T(8,128)} custom-call(f32[32,256]{1,0:T(8,128)} %values.1, f32[1,512]{1,0:T(1,128)} %bitcast.8), custom_call_target="tpu_custom_call" | custom-call | tf_op jit(solution)/shard_map/pallas_call | solution.py:24
  2.5 0.0 copy-start.1
  2.6 10.5 %all-to-all-start = ((f32[32,40,256]{2,1,0:T(8,128)}), f32[32,40,256]{2,1,0:T(8,128)S(1)}, u32[]{:S(2)}, u32[]{:S(2)}) async-start(f32[32,40,256]{2,1,0:T(8,128)} %shard_map.67), calls=%async_computation | async-start | bytes 2621440 | tf_op jit(solution)/shard_map/all_to_all | solution.py:239
  13.1 0.0 copy-done.1
  13.1 34.3 %all_gather.3.train = f32[512,256]{1,0:T(8,128)S(1)} all-gather(f32[32,256]{1,0:T(8,128)S(1)} %copy-done.1), channel_id=1, replica_groups={{0,33,64,97,128,161,192,225,256,289,320,353,384,417,448,481},{1,32,65,9..., dimensions={0}, use_global_device_ids=true | all-gather | bytes 557056 | tf_op jit(solution)/shard_map/all_gather | solution.py:240
  47.4 0.0 all-to-all-done
  47.4 0.1 broadcast_multiply_fusion.twice
  47.5 0.0 copy-start
  47.5 1.7 %shard_map.68 = (f32[1024,512]{1,0:T(8,128)S(1)}, f32[1,512]{1,0:T(1,128)S(1)}, f32[1,512]{1,0:T(1,128)S(1)}, f32[32,1,1024]{2,1,0:T(1,128)S(1)}) custom-call(f32[32,40,256]{2,1,0:T(8,128)S(1)} %broadcast_multiply_fusion.twice, f32[512,256]{1,0:T(8,128)S(1)} %all_gather.3.train), custom_call_target="tpu_custom_call" | custom-call | tf_op jit(solution)/shard_map/pallas_call | solution.py:24
  49.1 13.9 %all_to_all.40.got = f32[32,1,1024]{2,1,0:T(1,128)S(1)} all-to-all(f32[32,1,1024]{2,1,0:T(1,128)S(1)} %get-tuple-element.15), channel_id=1, replica_groups=mesh['gen'=16,'train'=32] {'train'}, dimensions={0} | all-to-all | bytes 262144 | tf_op jit(solution)/shard_map/all_to_all | solution.py:249
  63.0 0.0 copy-done
  63.0 0.6 shard_map.69
  63.6 18.0 %all_to_all.41.got = f32[16,1,512]{2,1,0:T(1,128)S(1)} all-to-all(f32[16,1,512]{2,1,0:T(1,128)S(1)} %shard_map.69), channel_id=1, replica_groups={{0,33,64,97,128,161,192,225,256,289,320,353,384,417,448,481},{1,32,65,9..., dimensions={0} | all-to-all | bytes 65536 | tf_op jit(solution)/shard_map/all_to_all | solution.py:256
  81.6 0.7 shard_map.70
  82.3 12.6 %all_to_all.42.got = f32[32,1,1024]{2,1,0:T(1,128)S(1)} all-to-all(f32[32,1,1024]{2,1,0:T(1,128)S(1)} %shard_map.70), channel_id=1, replica_groups=mesh['gen'=16,'train'=32] {'train'}, dimensions={0} | all-to-all | bytes 262144 | tf_op jit(solution)/shard_map/all_to_all | solution.py:249
  94.9 0.6 shard_map.71
  95.5 13.8 %all_to_all.43.got = f32[16,1,512]{2,1,0:T(1,128)S(1)} all-to-all(f32[16,1,512]{2,1,0:T(1,128)S(1)} %shard_map.71), channel_id=1, replica_groups={{0,33,64,97,128,161,192,225,256,289,320,353,384,417,448,481},{1,32,65,9..., dimensions={0} | all-to-all | bytes 65536 | tf_op jit(solution)/shard_map/all_to_all | solution.py:256
  109.4 0.7 shard_map.72
  110.1 12.5 %all_to_all.44.got = f32[32,1,1024]{2,1,0:T(1,128)S(1)} all-to-all(f32[32,1,1024]{2,1,0:T(1,128)S(1)} %shard_map.72), channel_id=1, replica_groups=mesh['gen'=16,'train'=32] {'train'}, dimensions={0} | all-to-all | bytes 262144 | tf_op jit(solution)/shard_map/all_to_all | solution.py:249
  122.6 0.8 shard_map.73
  123.4 14.4 %all_to_all.45.got = f32[16,1,1152]{2,1,0:T(1,128)S(1)} all-to-all(f32[16,1,1152]{2,1,0:T(1,128)S(1)} %get-tuple-element.18), channel_id=1, replica_groups={{0,33,64,97,128,161,192,225,256,289,320,353,384,417,448,481},{1,32,65,9..., dimensions={0} | all-to-all | bytes 147456 | tf_op jit(solution)/shard_map/all_to_all | solution.py:256
  137.8 0.1 shard_map.74
  137.9 12.5 %all_to_all.46.got = f32[32,1,768]{2,1,0:T(1,128)S(1)} all-to-all(f32[32,1,768]{2,1,0:T(1,128)S(1)} %get-tuple-element.20), channel_id=1, replica_groups=mesh['gen'=16,'train'=32] {'train'}, dimensions={0} | all-to-all | bytes 196608 | tf_op jit(solution)/shard_map/all_to_all | solution.py:265
  150.4 0.7 shard_map.75
Async XLA Ops:
  2.5 10.5 %copy-start.1 = (f32[32,256]{1,0:T(8,128)S(1)}, f32[32,256]{1,0:T(8,128)}, u32[]{:S(2)}) copy-start(f32[32,256]{1,0:T(8,128)} %param.5) | copy-start | bytes 98308
  2.6 44.8 %all-to-all-start = ((f32[32,40,256]{2,1,0:T(8,128)}), f32[32,40,256]{2,1,0:T(8,128)S(1)}, u32[]{:S(2)}, u32[]{:S(2)}) async-start(f32[32,40,256]{2,1,0:T(8,128)} %shard_map.67), calls=%async_computation | async-start | bytes 2621440 | tf_op jit(solution)/shard_map/all_to_all | solution.py:239
  47.5 15.6 %copy-start = (f32[1024]{0:T(1024)S(1)}, f32[1024]{0:T(1024)}, u32[]{:S(2)}) copy-start(f32[1024]{0:T(1024)} %param.6) | copy-start | bytes 12292

commit v10 on v9

--- a/solution.py
+++ b/solution.py
@@ -1,4 +1,5 @@
 import functools
+import math
 
 import jax
 import jax.numpy as jnp
@@ -11,6 +12,7 @@
 
 
 EPSILON = 0.05
+UNIT = EPSILON * math.log(2.0)
 LANES = 128
 VMEM = pl.BlockSpec(memory_space=pltpu.VMEM)
 ANY = pl.BlockSpec(memory_space=pl.ANY)
@@ -75,7 +77,7 @@
 def combined(got, cols):
     logs = [got[k, :, 0:cols] for k in range(got.shape[0])]
     highest = functools.reduce(jnp.maximum, logs)
-    return highest + jnp.log(sum(jnp.exp(log - highest) for log in logs))
+    return highest + jnp.log2(sum(jnp.exp2(log - highest) for log in logs))
 
 
 def row_logs(block, weights):
@@ -85,8 +87,8 @@
         return block[at : at + LANES, :] + weights
 
     highest = [jnp.max(scores(at), axis=1, keepdims=True) for at in starts]
-    totals = [jnp.sum(jnp.exp(scores(at) - high), axis=1, keepdims=True) for at, high in zip(starts, highest)]
-    logs = [high + jnp.log(total) for high, total in zip(highest, totals)]
+    totals = [jnp.sum(jnp.exp2(scores(at) - high), axis=1, keepdims=True) for at, high in zip(starts, highest)]
+    logs = [high + jnp.log2(total) for high, total in zip(highest, totals)]
     return [jnp.broadcast_to(log, (LANES, LANES)).T[0:1, :] for log in logs]
 
 
@@ -106,7 +108,7 @@
     potential = -combined(got, rows)
     if last:
         outs[0][...] = potential
-    weights = potential + jnp.log(mass[...])
+    weights = potential + jnp.log2(mass[...])
     lanes = cols // LANES
     sub = 8
 
@@ -124,12 +126,12 @@
     highest = jnp.max(highest, axis=0, keepdims=True)
     total = mean = jnp.zeros((sub, cols), jnp.float32)
     for at in range(0, rows, LANES):
-        share = jnp.exp(scores(at) - highest)
+        share = jnp.exp2(scores(at) - highest)
         total += fold(jnp.sum, share)
         if last:
             mean += fold(jnp.sum, share * affinity[at : at + LANES, :])
     total = jnp.sum(total, axis=0, keepdims=True)
-    logs = highest + jnp.log(total)
+    logs = highest + jnp.log2(total)
     if last:
         mean = jnp.sum(mean, axis=0, keepdims=True) / total
         masses = sum(mass[:, at : at + LANES] for at in range(0, rows, LANES))
@@ -149,7 +151,7 @@
 
     masses = jnp.where(own((1, cols)), mass_of(lax.axis_index("train")), mass_of(partner()))
     tile_mass[...] = masses
-    weights = jnp.log(masses)
+    weights = jnp.log2(masses)
     log_mass[...] = weights
     columns = halves(train[...])
     squares = [train[at : at + LANES, :] * train[at : at + LANES, :] for at in range(0, cols, LANES)]
@@ -179,11 +181,11 @@
     total = weighted = jnp.zeros_like(highest)
     sums = jnp.zeros_like(gen_mass)
     for k in range(count):
-        share = jnp.exp(logs[k] - highest)
+        share = jnp.exp2(logs[k] - highest)
         total += share
         weighted += share * got[k, :, cols : 2 * cols]
         sums += got[k, :, 2 * cols :]
-    potential = -(highest + jnp.log(total))
+    potential = -(highest + jnp.log2(total))
     col_pot[...] = potential
     gen_mass[...] = sums
     costs = mass[...] * (weighted / total)
@@ -202,11 +204,11 @@
     cost = jnp.sum(sums[:, 0:LANES], axis=1, keepdims=True)
     train_total = jnp.sum(sums[:, LANES:], axis=1, keepdims=True)
     columns = jnp.where(own(col_pot.shape), col_pot[...], got[partner(), :, 2 * LANES :])
-    log_train = jnp.log(train_total)
-    log_gen = jnp.log(jnp.sum(gen_mass[...], axis=1, keepdims=True))
-    row_out[...] = EPSILON * (row_pot[...] + (ITERS * log_train - (ITERS - 1) * log_gen))
-    col_out[...] = EPSILON * (columns + ITERS * (log_gen - log_train))
-    cost_out[...] = -EPSILON * cost / train_total
+    log_train = jnp.log2(train_total)
+    log_gen = jnp.log2(jnp.sum(gen_mass[...], axis=1, keepdims=True))
+    row_out[...] = UNIT * (row_pot[...] + (ITERS * log_train - (ITERS - 1) * log_gen))
+    col_out[...] = UNIT * (columns + ITERS * (log_gen - log_train))
+    cost_out[...] = -UNIT * cost / train_total
 
 
 def shards(n_gen, n_train, gen_embed, train_embed, row_mass, col_mass):
@@ -239,7 +241,7 @@
     twice = 2.0 * lax.all_to_all(packed, "train", 0, 0)
     train_block = lax.all_gather(train_embed, both, axis=0, tiled=True, axis_index_groups=groups)
     affinity, tile_mass, log_train, packed = call(
-        functools.partial(affinity_kernel, 1.0 / (width * EPSILON)),
+        functools.partial(affinity_kernel, 1.0 / (width * UNIT)),
         [shape(rows, cols), shape(1, cols), shape(1, cols), shape(n_train, 1, rows)],
         [twice, train_block],
     )

time: 152 us -> 152 us (level)
  no operation moved by 1% of the time
where the time goes in v10:
time: 152 us; the launch traced here: 151 us
  blocking collectives  132 us (87%)
  starting transfers between devices  10.5 us (7%)
  Pallas kernels  7.64 us (5%)
    all_to_all x4, blocking collectives, shards(): got = lax.all_to_all(packed, 'train', 0, 0)  51.5 us
    all_to_all x3, blocking collectives, shards(): got = lax.all_to_all(packed, both, 0, 0, axis_index_groups=groups)  46.2 us
    all_gather x1, blocking collectives, shards(): lax.all_gather(train_embed, both, axis=0, tiled=True, axis_index_groups=g...  34.3 us
    all_to_all x1, starting transfers between devices, shards(): twice = 2.0 * lax.all_to_all(packed, 'train', 0, 0)  10.5 us
    pallas_call x9, Pallas kernels, call(): pl.pallas_call(kernel, out_shape=outs, in_specs=in_specs or [VMEM] * len(...  7.64 us
  transfers between devices with their start and end apart: 1, of which 0 were waited for; matrix products, arithmetic and copies ran while one was open for 0% of the time, Pallas kernels for 0%

profile of v10, /device:TPU:1, one launch (start us, length us, event | category | flops | bytes accessed | tf_op | source)
XLA Modules:
  0.0 151.0 jit_solution(16724675331440439448)
XLA Ops:
  0.6 1.9 %shard_map.67 = f32[32,40,256]{2,1,0:T(8,128)} custom-call(f32[32,256]{1,0:T(8,128)} %values.1, f32[1,512]{1,0:T(1,128)} %bitcast.8), custom_call_target="tpu_custom_call" | custom-call | tf_op jit(solution)/shard_map/pallas_call | solution.py:26
  2.5 0.0 copy-start.1
  2.6 10.5 %all-to-all-start = ((f32[32,40,256]{2,1,0:T(8,128)}), f32[32,40,256]{2,1,0:T(8,128)S(1)}, u32[]{:S(2)}, u32[]{:S(2)}) async-start(f32[32,40,256]{2,1,0:T(8,128)} %shard_map.67), calls=%async_computation | async-start | bytes 2621440 | tf_op jit(solution)/shard_map/all_to_all | solution.py:241
  13.1 0.0 copy-done.1
  13.1 34.3 %all_gather.3.train = f32[512,256]{1,0:T(8,128)S(1)} all-gather(f32[32,256]{1,0:T(8,128)S(1)} %copy-done.1), channel_id=1, replica_groups={{0,33,64,97,128,161,192,225,256,289,320,353,384,417,448,481},{1,32,65,9..., dimensions={0}, use_global_device_ids=true | all-gather | bytes 557056 | tf_op jit(solution)/shard_map/all_gather | solution.py:242
  47.4 0.0 all-to-all-done
  47.4 0.1 broadcast_multiply_fusion.twice
  47.5 0.0 copy-start
  47.5 1.7 %shard_map.68 = (f32[1024,512]{1,0:T(8,128)S(1)}, f32[1,512]{1,0:T(1,128)S(1)}, f32[1,512]{1,0:T(1,128)S(1)}, f32[32,1,1024]{2,1,0:T(1,128)S(1)}) custom-call(f32[32,40,256]{2,1,0:T(8,128)S(1)} %broadcast_multiply_fusion.twice, f32[512,256]{1,0:T(8,128)S(1)} %all_gather.3.train), custom_call_target="tpu_custom_call" | custom-call | tf_op jit(solution)/shard_map/pallas_call | solution.py:26
  49.1 13.9 %all_to_all.40.got = f32[32,1,1024]{2,1,0:T(1,128)S(1)} all-to-all(f32[32,1,1024]{2,1,0:T(1,128)S(1)} %get-tuple-element.15), channel_id=1, replica_groups=mesh['gen'=16,'train'=32] {'train'}, dimensions={0} | all-to-all | bytes 262144 | tf_op jit(solution)/shard_map/all_to_all | solution.py:251
  63.0 0.0 copy-done
  63.0 0.6 shard_map.69
  63.6 18.0 %all_to_all.41.got = f32[16,1,512]{2,1,0:T(1,128)S(1)} all-to-all(f32[16,1,512]{2,1,0:T(1,128)S(1)} %shard_map.69), channel_id=1, replica_groups={{0,33,64,97,128,161,192,225,256,289,320,353,384,417,448,481},{1,32,65,9..., dimensions={0} | all-to-all | bytes 65536 | tf_op jit(solution)/shard_map/all_to_all | solution.py:258
  81.6 0.6 shard_map.70
  82.3 12.6 %all_to_all.42.got = f32[32,1,1024]{2,1,0:T(1,128)S(1)} all-to-all(f32[32,1,1024]{2,1,0:T(1,128)S(1)} %shard_map.70), channel_id=1, replica_groups=mesh['gen'=16,'train'=32] {'train'}, dimensions={0} | all-to-all | bytes 262144 | tf_op jit(solution)/shard_map/all_to_all | solution.py:251
  94.9 0.6 shard_map.71
  95.5 13.8 %all_to_all.43.got = f32[16,1,512]{2,1,0:T(1,128)S(1)} all-to-all(f32[16,1,512]{2,1,0:T(1,128)S(1)} %shard_map.71), channel_id=1, replica_groups={{0,33,64,97,128,161,192,225,256,289,320,353,384,417,448,481},{1,32,65,9..., dimensions={0} | all-to-all | bytes 65536 | tf_op jit(solution)/shard_map/all_to_all | solution.py:258
  109.3 0.6 shard_map.72
  110.0 12.5 %all_to_all.44.got = f32[32,1,1024]{2,1,0:T(1,128)S(1)} all-to-all(f32[32,1,1024]{2,1,0:T(1,128)S(1)} %shard_map.72), channel_id=1, replica_groups=mesh['gen'=16,'train'=32] {'train'}, dimensions={0} | all-to-all | bytes 262144 | tf_op jit(solution)/shard_map/all_to_all | solution.py:251
  122.5 0.8 shard_map.73
  123.3 14.4 %all_to_all.45.got = f32[16,1,1152]{2,1,0:T(1,128)S(1)} all-to-all(f32[16,1,1152]{2,1,0:T(1,128)S(1)} %get-tuple-element.18), channel_id=1, replica_groups={{0,33,64,97,128,161,192,225,256,289,320,353,384,417,448,481},{1,32,65,9..., dimensions={0} | all-to-all | bytes 147456 | tf_op jit(solution)/shard_map/all_to_all | solution.py:258
  137.7 0.1 shard_map.74
  137.8 12.5 %all_to_all.46.got = f32[32,1,768]{2,1,0:T(1,128)S(1)} all-to-all(f32[32,1,768]{2,1,0:T(1,128)S(1)} %get-tuple-element.20), channel_id=1, replica_groups=mesh['gen'=16,'train'=32] {'train'}, dimensions={0} | all-to-all | bytes 196608 | tf_op jit(solution)/shard_map/all_to_all | solution.py:267
  150.3 0.7 shard_map.75
Async XLA Ops:
  2.5 10.5 %copy-start.1 = (f32[32,256]{1,0:T(8,128)S(1)}, f32[32,256]{1,0:T(8,128)}, u32[]{:S(2)}) copy-start(f32[32,256]{1,0:T(8,128)} %param.5) | copy-start | bytes 98308
  2.6 44.8 %all-to-all-start = ((f32[32,40,256]{2,1,0:T(8,128)}), f32[32,40,256]{2,1,0:T(8,128)S(1)}, u32[]{:S(2)}, u32[]{:S(2)}) async-start(f32[32,40,256]{2,1,0:T(8,128)} %shard_map.67), calls=%async_computation | async-start | bytes 2621440 | tf_op jit(solution)/shard_map/all_to_all | solution.py:241
  47.5 15.6 %copy-start = (f32[1024]{0:T(1024)S(1)}, f32[1024]{0:T(1024)}, u32[]{:S(2)}) copy-start(f32[1024]{0:T(1024)} %param.6) | copy-start | bytes 12292

commit v11 on v10

--- a/solution.py
+++ b/solution.py
@@ -104,7 +104,7 @@
 
 def gen_kernel(last, got, mass, affinity, *outs):
     rows, cols = affinity.shape
-    out, offsets = outs[-2:]
+    out, held = outs[-2:]
     potential = -combined(got, rows)
     if last:
         outs[0][...] = potential
@@ -115,18 +115,17 @@
     def fold(reduce, block):
         return reduce(block.reshape(LANES // sub, sub, cols), axis=0)
 
-    def scores(at):
-        return affinity[at : at + LANES, :] + jnp.concatenate([offsets[at : at + LANES, :]] * lanes, axis=1)
-
     highest = None
     for at in range(0, rows, LANES):
-        offsets[at : at + LANES, :] = jnp.broadcast_to(weights[:, at : at + LANES], (LANES, LANES)).T
-        part = fold(jnp.max, scores(at))
+        offsets = jnp.broadcast_to(weights[:, at : at + LANES], (LANES, LANES)).T
+        scores = affinity[at : at + LANES, :] + jnp.concatenate([offsets] * lanes, axis=1)
+        held[at : at + LANES, :] = scores
+        part = fold(jnp.max, scores)
         highest = part if highest is None else jnp.maximum(highest, part)
     highest = jnp.max(highest, axis=0, keepdims=True)
     total = mean = jnp.zeros((sub, cols), jnp.float32)
     for at in range(0, rows, LANES):
-        share = jnp.exp2(scores(at) - highest)
+        share = jnp.exp2(held[at : at + LANES, :] - highest)
         total += fold(jnp.sum, share)
         if last:
             mean += fold(jnp.sum, share * affinity[at : at + LANES, :])
@@ -253,7 +252,7 @@
             functools.partial(gen_kernel, last),
             [shape(1, rows), shape(n_gen, 1, 2 * cols + LANES)] if last else [shape(n_gen, 1, cols)],
             [got, row_mass[None], affinity],
-            scratch=[pltpu.VMEM((rows, LANES), jnp.float32)],
+            scratch=[pltpu.VMEM((rows, cols), jnp.float32)],
         )
         got = lax.all_to_all(packed, both, 0, 0, axis_index_groups=groups)
         if not last:

time: 152 us -> 152 us (level)
  no operation moved by 1% of the time
where the time goes in v11:
time: 152 us; the launch traced here: 151 us
  blocking collectives  132 us (87%)
  starting transfers between devices  10.5 us (7%)
  Pallas kernels  7.63 us (5%)
    all_to_all x4, blocking collectives, shards(): got = lax.all_to_all(packed, 'train', 0, 0)  51.5 us
    all_to_all x3, blocking collectives, shards(): got = lax.all_to_all(packed, both, 0, 0, axis_index_groups=groups)  46.2 us
    all_gather x1, blocking collectives, shards(): lax.all_gather(train_embed, both, axis=0, tiled=True, axis_index_groups=g...  34.3 us
    all_to_all x1, starting transfers between devices, shards(): twice = 2.0 * lax.all_to_all(packed, 'train', 0, 0)  10.5 us
    pallas_call x9, Pallas kernels, call(): pl.pallas_call(kernel, out_shape=outs, in_specs=in_specs or [VMEM] * len(...  7.63 us
  transfers between devices with their start and end apart: 1, of which 0 were waited for; matrix products, arithmetic and copies ran while one was open for 0% of the time, Pallas kernels for 0%

profile of v11, /device:TPU:1, one launch (start us, length us, event | category | flops | bytes accessed | tf_op | source)
XLA Modules:
  0.0 151.0 jit_solution(6752475179022434886)
XLA Ops:
  0.6 1.9 %shard_map.67 = f32[32,40,256]{2,1,0:T(8,128)} custom-call(f32[32,256]{1,0:T(8,128)} %values.1, f32[1,512]{1,0:T(1,128)} %bitcast.8), custom_call_target="tpu_custom_call" | custom-call | tf_op jit(solution)/shard_map/pallas_call | solution.py:26
  2.5 0.0 copy-start.1
  2.6 10.5 %all-to-all-start = ((f32[32,40,256]{2,1,0:T(8,128)}), f32[32,40,256]{2,1,0:T(8,128)S(1)}, u32[]{:S(2)}, u32[]{:S(2)}) async-start(f32[32,40,256]{2,1,0:T(8,128)} %shard_map.67), calls=%async_computation | async-start | bytes 2621440 | tf_op jit(solution)/shard_map/all_to_all | solution.py:240
  13.1 0.0 copy-done.1
  13.1 34.3 %all_gather.3.train = f32[512,256]{1,0:T(8,128)S(1)} all-gather(f32[32,256]{1,0:T(8,128)S(1)} %copy-done.1), channel_id=1, replica_groups={{0,33,64,97,128,161,192,225,256,289,320,353,384,417,448,481},{1,32,65,9..., dimensions={0}, use_global_device_ids=true | all-gather | bytes 557056 | tf_op jit(solution)/shard_map/all_gather | solution.py:241
  47.4 0.0 all-to-all-done
  47.4 0.1 broadcast_multiply_fusion.twice
  47.5 0.0 copy-start
  47.5 1.7 %shard_map.68 = (f32[1024,512]{1,0:T(8,128)S(1)}, f32[1,512]{1,0:T(1,128)S(1)}, f32[1,512]{1,0:T(1,128)S(1)}, f32[32,1,1024]{2,1,0:T(1,128)S(1)}) custom-call(f32[32,40,256]{2,1,0:T(8,128)S(1)} %broadcast_multiply_fusion.twice, f32[512,256]{1,0:T(8,128)S(1)} %all_gather.3.train), custom_call_target="tpu_custom_call" | custom-call | tf_op jit(solution)/shard_map/pallas_call | solution.py:26
  49.1 13.9 %all_to_all.40.got = f32[32,1,1024]{2,1,0:T(1,128)S(1)} all-to-all(f32[32,1,1024]{2,1,0:T(1,128)S(1)} %get-tuple-element.15), channel_id=1, replica_groups=mesh['gen'=16,'train'=32] {'train'}, dimensions={0} | all-to-all | bytes 262144 | tf_op jit(solution)/shard_map/all_to_all | solution.py:250
  63.0 0.0 copy-done
  63.0 0.6 shard_map.69
  63.6 18.0 %all_to_all.41.got = f32[16,1,512]{2,1,0:T(1,128)S(1)} all-to-all(f32[16,1,512]{2,1,0:T(1,128)S(1)} %shard_map.69), channel_id=1, replica_groups={{0,33,64,97,128,161,192,225,256,289,320,353,384,417,448,481},{1,32,65,9..., dimensions={0} | all-to-all | bytes 65536 | tf_op jit(solution)/shard_map/all_to_all | solution.py:257
  81.6 0.6 shard_map.70
  82.3 12.6 %all_to_all.42.got = f32[32,1,1024]{2,1,0:T(1,128)S(1)} all-to-all(f32[32,1,1024]{2,1,0:T(1,128)S(1)} %shard_map.70), channel_id=1, replica_groups=mesh['gen'=16,'train'=32] {'train'}, dimensions={0} | all-to-all | bytes 262144 | tf_op jit(solution)/shard_map/all_to_all | solution.py:250
  94.9 0.6 shard_map.71
  95.5 13.8 %all_to_all.43.got = f32[16,1,512]{2,1,0:T(1,128)S(1)} all-to-all(f32[16,1,512]{2,1,0:T(1,128)S(1)} %shard_map.71), channel_id=1, replica_groups={{0,33,64,97,128,161,192,225,256,289,320,353,384,417,448,481},{1,32,65,9..., dimensions={0} | all-to-all | bytes 65536 | tf_op jit(solution)/shard_map/all_to_all | solution.py:257
  109.3 0.6 shard_map.72
  110.0 12.5 %all_to_all.44.got = f32[32,1,1024]{2,1,0:T(1,128)S(1)} all-to-all(f32[32,1,1024]{2,1,0:T(1,128)S(1)} %shard_map.72), channel_id=1, replica_groups=mesh['gen'=16,'train'=32] {'train'}, dimensions={0} | all-to-all | bytes 262144 | tf_op jit(solution)/shard_map/all_to_all | solution.py:250
  122.5 0.8 shard_map.73
  123.3 14.4 %all_to_all.45.got = f32[16,1,1152]{2,1,0:T(1,128)S(1)} all-to-all(f32[16,1,1152]{2,1,0:T(1,128)S(1)} %get-tuple-element.18), channel_id=1, replica_groups={{0,33,64,97,128,161,192,225,256,289,320,353,384,417,448,481},{1,32,65,9..., dimensions={0} | all-to-all | bytes 147456 | tf_op jit(solution)/shard_map/all_to_all | solution.py:257
  137.7 0.1 shard_map.74
  137.8 12.5 %all_to_all.46.got = f32[32,1,768]{2,1,0:T(1,128)S(1)} all-to-all(f32[32,1,768]{2,1,0:T(1,128)S(1)} %get-tuple-element.20), channel_id=1, replica_groups=mesh['gen'=16,'train'=32] {'train'}, dimensions={0} | all-to-all | bytes 196608 | tf_op jit(solution)/shard_map/all_to_all | solution.py:266
  150.3 0.7 shard_map.75
Async XLA Ops:
  2.5 10.5 %copy-start.1 = (f32[32,256]{1,0:T(8,128)S(1)}, f32[32,256]{1,0:T(8,128)}, u32[]{:S(2)}) copy-start(f32[32,256]{1,0:T(8,128)} %param.5) | copy-start | bytes 98308
  2.6 44.8 %all-to-all-start = ((f32[32,40,256]{2,1,0:T(8,128)}), f32[32,40,256]{2,1,0:T(8,128)S(1)}, u32[]{:S(2)}, u32[]{:S(2)}) async-start(f32[32,40,256]{2,1,0:T(8,128)} %shard_map.67), calls=%async_computation | async-start | bytes 2621440 | tf_op jit(solution)/shard_map/all_to_all | solution.py:240
  47.5 15.6 %copy-start = (f32[1024]{0:T(1024)S(1)}, f32[1024]{0:T(1024)}, u32[]{:S(2)}) copy-start(f32[1024]{0:T(1024)} %param.6) | copy-start | bytes 12292
